TPU v7x, 32 devices: a whole 2x2x4 slice. The times are simulated.
32 devices in a mesh: morton: 8 (over z, y), sub: 4 (over x, core).
Axes of the slice: x: 2, y: 2, z: 4, core: 2. Of those that a mesh axis runs over, the one named last changes fastest.
Arguments:
- multipoles: bfloat16 [2048, 128], P(('morton', 'sub')), may hold values from -6 to 6
- translations: bfloat16 [316, 128, 128], P('sub'), may hold values from -0.0625 to 0.0625
- upward_ops: bfloat16 [8, 128, 128], replicated, may hold values from -0.1875 to 0.1875
- downward_ops: bfloat16 [8, 128, 128], replicated, may hold values from -0.375 to 0.375
- targets_l6: int32 [8, 316, 128], P('morton', 'sub'), may hold values from 0 to 255, as said below
- source_boxes_level6: int32 [8, 316, 128], P('morton', 'sub'), may hold values from 0 to 767, as said below
- counts_l6: int32 [8, 316], P('morton', 'sub'), may hold values from 1 to 128, as said below
- target_boxes_level5: int32 [8, 316, 16], P('morton', 'sub'), may hold values from 0 to 31, as said below
- anchors_l5: int32 [8, 316, 16], P('morton', 'sub'), may hold values from 0 to 255, as said below
- counts_l5: int32 [8, 316], P('morton', 'sub'), may hold values from 1 to 16, as said below
- targets_l4: int32 [8, 316, 2], P('morton', 'sub'), may hold values from 0 to 3, as said below
- anchors_l4: int32 [8, 316, 2], P('morton', 'sub'), may hold values from 0 to 31, as said below
- counts_l4: int32 [8, 316], P('morton', 'sub'), may hold values from 1 to 2, as said below
Outputs:
- local_exp: bfloat16 [2048, 128], P(('morton', 'sub'))
Inputs may be any that keep to these rules, and one draw needn't show every extreme that they name: `targets_l6`: targets of one operator's block within one subtree are its level-6 boxes. `source_boxes_level6`: sources lie in the previous, own or next subtree, at most 256 boxes before or after the target. `counts_l6`: some block of every subtree is full. `target_boxes_level5`: targets are level-5 boxes of the subtree. `anchors_l5`: sources are level-5 boxes of the aligned group of 8 subtrees. `counts_l5`: some block of every subtree is full. `targets_l4`: targets are level-4 boxes of the subtree. `anchors_l4`: sources are level-4 boxes of the aligned group of 8 subtrees. `counts_l4`: some block of every subtree is full.
All inputs are finite; a program needn't handle non-finite values.
Results may differ from a plain program's by a relative error of at most 0.011.
Values may be sent and summed in bfloat16 or wider, within the bound.
A program may use at most 64 MiB of HBM per device.

v0:
```python
import jax
import jax.numpy as jnp
from jax import lax
from jax.sharding import PartitionSpec as P


def swapped(shard, axis, apart):
    return lax.ppermute(shard, axis, [(i, i ^ 1 << apart) for i in range(lax.axis_size(axis))])


def with_halo(shard, sides, width):
    for axis, dim in sides:
        size, length = (lax.axis_size(axis), shard.shape[dim])
        up = [(i, (i + 1) % size) for i in range(size - 1)]
        down = [(j, i) for i, j in up]
        last = lax.slice_in_dim(shard, length - width, length, axis=dim)
        leading = lax.slice_in_dim(shard, 0, width, axis=dim)
        before = lax.ppermute(last, axis, up)
        after = lax.ppermute(leading, axis, down)
        shard = jnp.concatenate([before, shard, after], axis=dim)
    return shard


def translate_block(expansions, targets, anchors, counts, kernels, row_count, factor):
    operator_matrices, capacity = targets.shape
    coeff_width = expansions.shape[1]
    block_rows = min(capacity, 128)
    turn_count = capacity // block_rows
    target_steps = targets.reshape(operator_matrices, turn_count, block_rows).transpose(1, 0, 2)
    anchor_steps = anchors.reshape(operator_matrices, turn_count, block_rows).transpose(1, 0, 2)
    slot_steps = jnp.arange(capacity, dtype=jnp.int32).reshape(turn_count, block_rows)
    source_ids = jnp.arange(expansions.shape[0], dtype=jnp.int32)
    row_ids = jnp.arange(row_count, dtype=jnp.int32)

    def single_rotation(totals, inputs):
        target_rows, anchor_rows, slot_numbers = inputs
        selector = (anchor_rows.reshape(-1)[:, None] == source_ids[None, :]).astype(jnp.bfloat16)
        picked = jnp.dot(selector, expansions, preferred_element_type=jnp.float32).astype(
            jnp.bfloat16
        )
        picked = picked.reshape(operator_matrices, block_rows, coeff_width)
        product = jnp.einsum("obr,ors->obs", picked, kernels, preferred_element_type=jnp.float32)
        is_live = (slot_numbers[None, :] < counts[:, None]).reshape(-1)
        placing = jnp.logical_and(
            target_rows.reshape(-1)[:, None] == row_ids[None, :], is_live[:, None]
        )
        placing = placing.astype(jnp.float32) * factor
        added = jnp.einsum(
            "kt,kc->tc",
            placing,
            product.reshape(-1, coeff_width),
            precision=lax.Precision.HIGHEST,
            preferred_element_type=jnp.float32,
        )
        return (totals + added, None)

    totals, _ = lax.scan(
        single_rotation,
        jnp.zeros((row_count, coeff_width), jnp.float32),
        (target_steps, anchor_steps, slot_steps),
    )
    return totals


def upward(children, operator_matrices):
    parents = children.shape[0] // 8
    grouped_rows = children.reshape(parents, 8, children.shape[1])
    summed_values = jnp.einsum(
        "duo,uob->db", grouped_rows, operator_matrices, preferred_element_type=jnp.float32
    )
    return summed_values.astype(jnp.bfloat16)


def downward(parent, operator_matrices):
    spread = jnp.einsum(
        "pr,crs->pcs", parent, operator_matrices, preferred_element_type=jnp.float32
    )
    return spread.reshape(-1, parent.shape[1])


def gather_group(pieces):
    joined = (
        lax.all_gather(pieces[0], "sub", axis=0, tiled=True),
        lax.all_gather(pieces[1], "sub", axis=0, tiled=True),
    )
    position = lax.axis_index("morton")
    for level_bit in range(3):
        packed = jnp.concatenate(joined, axis=0)
        partner = swapped(packed, "morton", level_bit)
        is_upper = position >> level_bit & 1 == 1
        offset = 0
        updated = []
        for own_rows in joined:
            theirs = partner[offset : offset + own_rows.shape[0]]
            offset = offset + own_rows.shape[0]
            updated.append(
                jnp.where(
                    is_upper,
                    jnp.concatenate([theirs, own_rows], axis=0),
                    jnp.concatenate([own_rows, theirs], axis=0),
                )
            )
        joined = tuple(updated)
    return joined


def local(
    multipoles,
    translations,
    upward_ops,
    downward_ops,
    targets_l6,
    source_boxes_level6,
    counts_l6,
    target_boxes_level5,
    anchors_l5,
    counts_l5,
    targets_l4,
    anchors_l4,
    counts_l4,
):
    quarter = multipoles.shape[0]
    sub_count = lax.axis_size("sub")
    box_count = quarter * sub_count
    anchor_rows = source_boxes_level6[0]
    with_rims = with_halo(multipoles, (("morton", 0),), quarter)
    nearby = lax.all_gather(with_rims, "sub", axis=0, tiled=True)
    block_index = anchor_rows // box_count
    within = anchor_rows % box_count
    anchor_rows = within // quarter * (3 * quarter) + block_index * quarter + within % quarter
    partial_six = translate_block(
        nearby, targets_l6[0], anchor_rows, counts_l6[0], translations, box_count, 1.0
    )
    far_six = lax.psum_scatter(
        partial_six.astype(jnp.bfloat16), "sub", scatter_dimension=0, tiled=True
    ).astype(jnp.float32)
    coarse5 = upward(multipoles, upward_ops)
    coarse4 = upward(coarse5, upward_ops)
    group_five, group_four = gather_group((coarse5, coarse4))
    partial_five = translate_block(
        group_five,
        target_boxes_level5[0],
        anchors_l5[0],
        counts_l5[0],
        translations,
        box_count // 8,
        0.5,
    )
    partial_four = translate_block(
        group_four, targets_l4[0], anchors_l4[0], counts_l4[0], translations, box_count // 64, 0.25
    )
    far_five, far_four = (
        lax.psum_scatter(partial_five, "sub", scatter_dimension=0, tiled=True),
        lax.psum_scatter(partial_four, "sub", scatter_dimension=0, tiled=True),
    )
    local4 = far_four.astype(jnp.bfloat16)
    local5 = (far_five + downward(local4, downward_ops)).astype(jnp.bfloat16)
    return (far_six + downward(local5, downward_ops)).astype(jnp.bfloat16)


def solution(mesh):
    placed = (
        P(("morton", "sub"), None),
        P("sub", None, None),
        P(),
        P(),
        P("morton", "sub", None),
        P("morton", "sub", None),
        P("morton", "sub"),
        P("morton", "sub", None),
        P("morton", "sub", None),
        P("morton", "sub"),
        P("morton", "sub", None),
        P("morton", "sub", None),
        P("morton", "sub"),
    )
    return jax.shard_map(
        local, mesh=mesh, in_specs=placed, out_specs=P(("morton", "sub"), None), check_vma=False
    )
```

profile of v0, /device:TPU:0, one launch (start us, length us, event | category | flops | bytes accessed | tf_op | source)
XLA Modules:
  0.0 99.6 jit_solution(13233136187264449810)
XLA Ops:
  6.5 5.1 %collective-permute-start = (bf16[64,128]{1,0:T(8,128)(2,1)}, bf16[64,128]{1,0:T(8,128)(2,1)S(1)}, u32[]{:S(2)}, u32[]{:S(2)}) collective-permute-start(bf16[64,128]{1,0:T(8,128)(2,1)} %param.13), channel_id=1, source_target_pairs={{0,4},{4,8},{8,12},{12,16},{16,20},{20,24},{24,28},{1,5},{5,9},{9,... | collective-permute-start | bytes 49160 | tf_op jit(solution)/shard_map/ppermute | solution.py:18
  11.7 1.3 %collective-permute-start.1 = (bf16[64,128]{1,0:T(8,128)(2,1)}, bf16[64,128]{1,0:T(8,128)(2,1)S(1)}, u32[]{:S(2)}, u32[]{:S(2)}) collective-permute-start(bf16[64,128]{1,0:T(8,128)(2,1)} %param.13), channel_id=1, source_target_pairs={{4,0},{8,4},{12,8},{16,12},{20,16},{24,20},{28,24},{5,1},{9,5},{13... | collective-permute-start | bytes 49160 | tf_op jit(solution)/shard_map/ppermute | solution.py:19
  13.0 1.1 %fusion.11 = bf16[8,128]{1,0:T(8,128)(2,1)S(1)} fusion(bf16[8,128,128]{2,1,0:T(8,128)(2,1)} %param.15, bf16[8,8,128]{2,1,0:T(8,128)(2,1)} %bitcast.77), kind=kOutput, calls=%fused_computation.14 | convolution fusion | flops 2098176 | bytes 280576 | tf_op jit(solution)/shard_map/duo,uob->db/dot_general | solution.py:68
  14.1 5.2 %all_gather.10 = bf16[32,128]{1,0:T(8,128)(2,1)S(1)} all-gather(bf16[8,128]{1,0:T(8,128)(2,1)S(1)} %fusion.11), channel_id=1, replica_groups=mesh['morton'=8,'sub'=4] {'sub'}, dimensions={0}, use_global_device_ids=true | all-gather | bytes 10240 | tf_op jit(solution)/shard_map/all_gather | solution.py:83
  19.2 1.1 %fusion.13 = bf16[1,1,128]{2,1,0:T(2,128)(2,1)S(1)} fusion(bf16[8,128,128]{2,1,0:T(8,128)(2,1)} %param.15, bf16[8,128,1]{1,0,2:T(8,128)(2,1)S(1)} %bitcast.79), kind=kOutput, calls=%fused_computation.17 | convolution fusion | flops 262272 | bytes 264448 | tf_op jit(solution)/shard_map/duo,uob->db/dot_general | solution.py:68
  20.3 5.0 %all-gather.1 = bf16[4,1,128]{2,1,0:T(2,128)(2,1)S(1)} all-gather(bf16[1,1,128]{2,1,0:T(2,128)(2,1)S(1)} %fusion.13), channel_id=2, replica_groups=mesh['morton'=8,'sub'=4] {'sub'}, dimensions={0}, use_global_device_ids=true | all-gather | bytes 1280 | tf_op jit(solution)/shard_map/all_gather | solution.py:84
  25.4 2.7 %collective-permute-start.2 = (bf16[36,128]{1,0:T(8,128)(2,1)S(1)}, bf16[36,128]{1,0:T(8,128)(2,1)S(1)}, u32[]{:S(2)}, u32[]{:S(2)}) collective-permute-start(bf16[36,128]{1,0:T(8,128)(2,1)S(1)} %pad_maximum_fusion.3), channel_id=1, source_target_pairs={{0,4},{4,0},{8,12},{12,8},{16,20},{20,16},{24,28},{28,24},{1,5},{5... | collective-permute-start | bytes 27656 | tf_op jit(solution)/shard_map/ppermute | solution.py:8
  28.8 0.9 reduce.1
  29.8 0.7 fusion.45
  30.5 0.7 iota_compare_fusion.11
  31.3 0.8 copy.31
  32.2 0.8 copy.30
  33.2 0.8 copy.34
  34.6 0.8 copy.33
  36.3 0.9 reduce
  37.2 1.3 %dynamic-slice.1 = u32[1]{0:T(128)} dynamic-slice(u32[32]{0:T(128)} %constant.112, u32[]{:T(128)S(6)} %add.55), dynamic_slice_sizes={1} | dynamic-slice | bytes 12
  39.2 1.6 %collective-permute-start.3 = (bf16[72,128]{1,0:T(8,128)(2,1)S(1)}, bf16[72,128]{1,0:T(8,128)(2,1)S(1)}, u32[]{:S(2)}, u32[]{:S(2)}) collective-permute-start(bf16[72,128]{1,0:T(8,128)(2,1)S(1)} %pad_maximum_fusion.2), channel_id=1, source_target_pairs={{0,8},{4,12},{8,0},{12,4},{16,24},{20,28},{24,16},{28,20},{1,9},{5... | collective-permute-start | bytes 55304 | tf_op jit(solution)/shard_map/ppermute | solution.py:8
  41.5 5.6 %all_gather.9 = bf16[768,128]{1,0:T(8,128)(2,1)S(1)} all-gather(bf16[192,128]{1,0:T(8,128)(2,1)S(1)} %pad_maximum_fusion), channel_id=1, replica_groups=mesh['morton'=8,'sub'=4] {'sub'}, dimensions={0}, use_global_device_ids=true | all-gather | bytes 245760 | tf_op jit(solution)/shard_map/all_gather | solution.py:127
  47.1 7.6 %fusion.2 = bf16[10112,128]{1,0:T(8,128)(2,1)S(1)} fusion(bf16[768,128]{1,0:T(8,128)(2,1)S(1)} %all_gather.9, s32[10112]{0:T(1024)S(1)} %fusion.35), kind=kOutput, calls=%fused_computation.3 | convolution fusion | flops 1997160448 | bytes 2825728 | tf_op jit(solution)/shard_map/while/body/eval_jaxpr/dot_general | solution.py:38
  54.8 0.8 fusion.74
  55.7 2.6 %collective-permute-start.4 = (bf16[144,128]{1,0:T(8,128)(2,1)S(1)}, bf16[144,128]{1,0:T(8,128)(2,1)S(1)}, u32[]{:S(2)}, u32[]{:S(2)}) collective-permute-start(bf16[144,128]{1,0:T(8,128)(2,1)S(1)} %pad_maximum_fusion.1), channel_id=1, source_target_pairs={{0,16},{4,20},{8,24},{12,28},{16,0},{20,4},{24,8},{28,12},{1,17},{... | collective-permute-start | bytes 110600 | tf_op jit(solution)/shard_map/ppermute | solution.py:8
  58.3 11.6 %fusion.8 = bf16[256,128]{1,0:T(8,128)(2,1)} fusion(f32[10112,128]{1,0:T(8,128)S(1)} %bitcast.73, s32[10112]{0:T(1024)S(1)} %bitcast.78, pred[10112]{0:T(1024)(128)(4,1)S(1)} %fusion.45), kind=kOutput, calls=%fused_computation.11 | convolution fusion | flops 3981410304 | bytes 5293440 | tf_op jit(solution)/shard_map/while/body/eval_jaxpr/kt,kc->tc/dot_general | solution.py:48
  70.4 1.0 %fusion.75 = f32[79,16,128]{2,1,0:T(8,128)S(1)} fusion(bf16[79,16,128]{2,1,0:T(8,128)(2,1)S(1)} %bitcast.76, bf16[79,128,128]{2,1,0:T(8,128)(2,1)S(1)} %copy-done), kind=kOutput, calls=%fused_computation.108 | convolution fusion | flops 41418752 | bytes 3559424 | tf_op jit(solution)/shard_map/while/body/eval_jaxpr/obr,ors->obs/dot_general | solution.py:42
  71.4 1.6 %convolution_convert_fusion.1 = bf16[158,128]{1,0:T(8,128)(2,1)} fusion(s32[158]{0:T(256)} %eq.164, bf16[16,128]{1,0:T(8,128)(2,1)S(1)} %maximum_select_fusion.6, bf16[16,128]{1,0:T(8,128)(2,1)S(1)} %slice.29, pred[]{:T(512)S(6)} %eq.157), kind=kOutput, calls=%fused_computation.12 | convolution fusion | flops 1356480 | bytes 49273 | tf_op jit(solution)/shard_map/while/body/eval_jaxpr/dot_general | solution.py:38
  73.0 0.8 reshape.127
  73.8 1.4 %fusion.76 = f32[79,2,128]{2,1,0:T(2,128)} fusion(bf16[79,2,128]{2,1,0:T(2,128)(2,1)S(1)} %reshape.127, bf16[79,128,128]{2,1,0:T(8,128)(2,1)S(1)} %copy-done), kind=kOutput, calls=%fused_computation.109 | convolution fusion | flops 5177344 | bytes 2710016 | tf_op jit(solution)/shard_map/while/body/eval_jaxpr/obr,ors->obs/dot_general | solution.py:42
  75.2 1.6 %reshape.128 = f32[158,128]{1,0:T(8,128)} reshape(f32[79,2,128]{2,1,0:T(2,128)} %fusion.76) | data formatting | bytes 161792 | tf_op jit(solution)/shard_map/while/body/eval_jaxpr/reshape | solution.py:51
  76.8 1.1 %fusion.15 = f32[32,128]{1,0:T(8,128)S(1)} fusion(f32[1264,128]{1,0:T(8,128)S(1)} %bitcast.75, s32[1264]{0:T(1024)S(1)} %eq.149, pred[1264]{0:T(1024)(128)(4,1)S(1)} %lt.111), kind=kOutput, calls=%fused_computation.19 | convolution fusion | flops 62249472 | bytes 669872 | tf_op jit(solution)/shard_map/while/body/eval_jaxpr/kt,kc->tc/dot_general | solution.py:48
  77.9 1.2 %fusion.23 = f32[4,128]{1,0:T(4,128)S(1)} fusion(f32[158,128]{1,0:T(8,128)} %reshape.128, s32[158]{0:T(256)S(1)} %eq.160, pred[158]{0:T(512)(128)(4,1)} %lt.116), kind=kOutput, calls=%fused_computation.28 | convolution fusion | flops 972648 | bytes 83734 | tf_op jit(solution)/shard_map/while/body/eval_jaxpr/kt,kc->tc/dot_general | solution.py:48
  79.1 11.3 %all-reduce.2 = (bf16[4,128]{1,0:T(4,128)(2,1)S(1)}, f32[32,128]{1,0:T(8,128)S(1)}) all-reduce(f32[4,128]{1,0:T(4,128)S(1)} %fusion.23, f32[32,128]{1,0:T(8,128)S(1)} %fusion.15), channel_id=5, replica_groups=mesh['morton'=8,'sub'=4] {'sub'}, use_global_device_ids=true, to_apply=%region_2.3.clone | all-reduce | flops 4608 | bytes 35840
  90.4 0.8 fusion.66
  91.4 1.3 %fusion.50 = bf16[64,128]{1,0:T(8,128)(2,1)} fusion(f32[8,8,128]{2,0,1:T(8,128)S(1)} %fusion.61, bf16[64,128]{1,0:T(8,128)(2,1)} %reduce-scatter.2.cloned.1.call-done), kind=kLoop, calls=%fused_computation.76 | loop fusion | flops 24576 | bytes 65536 | tf_op jit(solution)/shard_map/convert_element_type | solution.py:158
  (37 shorter events, 4.0 us)
Async XLA Ops:
  6.5 48.2 %copy-start = (bf16[79,128,128]{2,1,0:T(8,128)(2,1)S(1)}, bf16[79,128,128]{2,1,0:T(8,128)(2,1)}, u32[]{:S(2)}) copy-start(bf16[79,128,128]{2,1,0:T(8,128)(2,1)} %param.14) | copy-start | bytes 7766020
  6.5 84.8 %reduce-scatter.2.cloned.1.call-start = ((), (), s32[]{:S(2)}) async-start(), calls=%async_computation.1 | async-start | bytes 81920 | tf_op jit(solution)/shard_map/reduce_scatter | solution.py:134
  6.5 34.3 %collective-permute-start = (bf16[64,128]{1,0:T(8,128)(2,1)}, bf16[64,128]{1,0:T(8,128)(2,1)S(1)}, u32[]{:S(2)}, u32[]{:S(2)}) collective-permute-start(bf16[64,128]{1,0:T(8,128)(2,1)} %param.13), channel_id=1, source_target_pairs={{0,4},{4,8},{8,12},{12,16},{16,20},{20,24},{24,28},{1,5},{5,9},{9,... | collective-permute-start | bytes 49160 | tf_op jit(solution)/shard_map/ppermute | solution.py:18
  11.7 29.1 %collective-permute-start.1 = (bf16[64,128]{1,0:T(8,128)(2,1)}, bf16[64,128]{1,0:T(8,128)(2,1)S(1)}, u32[]{:S(2)}, u32[]{:S(2)}) collective-permute-start(bf16[64,128]{1,0:T(8,128)(2,1)} %param.13), channel_id=1, source_target_pairs={{4,0},{8,4},{12,8},{16,12},{20,16},{24,20},{28,24},{5,1},{9,5},{13... | collective-permute-start | bytes 49160 | tf_op jit(solution)/shard_map/ppermute | solution.py:19
  25.4 13.7 %collective-permute-start.2 = (bf16[36,128]{1,0:T(8,128)(2,1)S(1)}, bf16[36,128]{1,0:T(8,128)(2,1)S(1)}, u32[]{:S(2)}, u32[]{:S(2)}) collective-permute-start(bf16[36,128]{1,0:T(8,128)(2,1)S(1)} %pad_maximum_fusion.3), channel_id=1, source_target_pairs={{0,4},{4,0},{8,12},{12,8},{16,20},{20,16},{24,28},{28,24},{1,5},{5... | collective-permute-start | bytes 27656 | tf_op jit(solution)/shard_map/ppermute | solution.py:8
  39.2 16.4 %collective-permute-start.3 = (bf16[72,128]{1,0:T(8,128)(2,1)S(1)}, bf16[72,128]{1,0:T(8,128)(2,1)S(1)}, u32[]{:S(2)}, u32[]{:S(2)}) collective-permute-start(bf16[72,128]{1,0:T(8,128)(2,1)S(1)} %pad_maximum_fusion.2), channel_id=1, source_target_pairs={{0,8},{4,12},{8,0},{12,4},{16,24},{20,28},{24,16},{28,20},{1,9},{5... | collective-permute-start | bytes 55304 | tf_op jit(solution)/shard_map/ppermute | solution.py:8
  55.7 14.3 %collective-permute-start.4 = (bf16[144,128]{1,0:T(8,128)(2,1)S(1)}, bf16[144,128]{1,0:T(8,128)(2,1)S(1)}, u32[]{:S(2)}, u32[]{:S(2)}) collective-permute-start(bf16[144,128]{1,0:T(8,128)(2,1)S(1)} %pad_maximum_fusion.1), channel_id=1, source_target_pairs={{0,16},{4,20},{8,24},{12,28},{16,0},{20,4},{24,8},{28,12},{1,17},{... | collective-permute-start | bytes 110600 | tf_op jit(solution)/shard_map/ppermute | solution.py:8
  71.4 19.0 %copy-start.1 = (bf16[8,128,128]{2,1,0:T(8,128)(2,1)S(1)}, bf16[8,128,128]{2,1,0:T(8,128)(2,1)}, u32[]{:S(2)}) copy-start(bf16[8,128,128]{2,1,0:T(8,128)(2,1)} %param.16) | copy-start | bytes 786436
Sparse Core Ops, SparseCore 0:
  70.1 17.5 reduce-scatter.1
where the time goes:
time: 100 us; the launch traced here: 99.6 us
  matrix products  29.9 us (30%)
  blocking collectives  27.1 us (27%)
  between operations  14.3 us (14%)
  starting transfers between devices  13.4 us (13%)
  local copies, waits for them, and re-layouts  8.67 us (9%)
  other arithmetic  6.15 us (6%)
    dot_general x3, matrix products, single_rotation(): jnp.einsum('kt,kc->tc', placing, product.reshape(-1, coeff_width), precis...  14 us
    unnamed x1, blocking collectives  11.3 us
    dot_general x3, matrix products, single_rotation(): jnp.dot(selector, expansions, preferred_element_type=jnp.float32)  9.55 us
    ppermute x3, starting transfers between devices, swapped(): lax.ppermute(shard, axis, [(i, i ^ 1 << apart) for i in range(lax.axis_si...  7 us
    all_gather x1, blocking collectives, local(): nearby = lax.all_gather(with_rims, 'sub', axis=0, tiled=True)  5.59 us
    all_gather x1, blocking collectives, gather_group(): lax.all_gather(pieces[0], 'sub', axis=0, tiled=True)  5.16 us
    ppermute x1, starting transfers between devices, with_halo(): before = lax.ppermute(last, axis, up)  5.12 us
    all_gather x1, blocking collectives, gather_group(): lax.all_gather(pieces[1], 'sub', axis=0, tiled=True)  5.03 us
  transfers between devices with their start and end apart: 6, of which 0 were waited for; matrix products, arithmetic and copies ran while one was open for 44% of the time, Pallas kernels for 0%

commit v1 on v0

v1 whole, which is shorter than its diff:
```python
import functools

import jax
import jax.numpy as jnp
from jax import lax
from jax.experimental import pallas as pl
from jax.experimental.pallas import tpu as pltpu
from jax.sharding import PartitionSpec as P

BF16 = jnp.bfloat16
F32 = jnp.float32
MESH = pl.DeviceIdType.MESH
GROUP = 8
PACK = 16
STEP = 16


def dot(a, b):
    return jnp.dot(a, b, preferred_element_type=F32)


def dot_nt(a, b):
    return lax.dot_general(a, b, (((1,), (1,)), ((), ())), preferred_element_type=F32)


def upward_into(mult_ref, up_ref, wide, pack):
    parents = mult_ref.shape[0] // 8
    wide[...] = mult_ref[...].astype(F32)
    children = [wide[pl.ds(c, parents, stride=8), :] for c in range(8)]
    lhs = jnp.concatenate(children, axis=1).astype(BF16)
    ops = up_ref[...].reshape(-1, up_ref.shape[2])
    five = dot(lhs, ops).astype(BF16).astype(F32)
    row = jnp.concatenate([five[c : c + 1, :] for c in range(8)], axis=1).astype(BF16)
    four = dot(row, ops)
    pad = jnp.zeros((PACK - parents - 1, five.shape[1]), F32)
    pack[...] = jnp.concatenate([five, four, pad], axis=0).astype(BF16)


def peers_of(sizes):
    n_m, n_s = sizes
    m, s = lax.axis_index("morton"), lax.axis_index("sub")
    base = m // GROUP * GROUP
    mine = (m - base) * n_s + s

    def group_peer(k):
        slot = (mine + k) % (GROUP * n_s)
        return slot, (base + slot // n_s, slot % n_s)

    def halo_peer(k):
        shift = k // n_s * 2 - 1
        return shift, ((m + shift + n_m) % n_m, k % n_s)

    return m, s, mine, group_peer, halo_peer


def exchange_kernel(
    sizes, mult_ref, up_ref, near_ref, coarse_ref, wide, pack,
    near_send, near_recv, coarse_send, coarse_recv,
):
    n_m, n_s = sizes
    m, s, mine, group_peer, halo_peer = peers_of(sizes)
    slots = GROUP * n_s
    upward_into(mult_ref, up_ref, wide, pack)

    barrier = pltpu.get_barrier_semaphore()

    def greet(k, _):
        pl.semaphore_signal(barrier, inc=1, device_id=group_peer(k)[1], device_id_type=MESH)
        return 0

    def greet_halo(k, _):
        pl.semaphore_signal(barrier, inc=1, device_id=halo_peer(k)[1], device_id_type=MESH)
        return 0

    lax.fori_loop(1, slots, greet, 0)
    expected = slots - 1
    if n_m > GROUP:
        lax.fori_loop(0, 2 * n_s, greet_halo, 0)
        expected = expected + 2 * n_s
    pl.semaphore_wait(barrier, expected)

    def coarse_copy(k, there):
        slot, peer = group_peer(k)
        return pltpu.make_async_remote_copy(
            src_ref=pack,
            dst_ref=coarse_ref.at[slot if there else mine],
            send_sem=coarse_send.at[k],
            recv_sem=coarse_recv.at[slot if there else mine],
            device_id=peer,
            device_id_type=MESH,
        )

    def sub_copy(k, there):
        other = (s + k) % n_s
        lands = n_s + (other if there else s)
        return pltpu.make_async_remote_copy(
            src_ref=mult_ref,
            dst_ref=near_ref.at[lands],
            send_sem=near_send.at[2 * n_s + k],
            recv_sem=near_recv.at[lands],
            device_id=(m, other),
            device_id_type=MESH,
        )

    def halo_copy(k, there):
        shift, peer = halo_peer(k)
        lands = (1 + shift) * n_s + peer[1] if there else (1 - shift) * n_s + s
        return pltpu.make_async_remote_copy(
            src_ref=mult_ref,
            dst_ref=near_ref.at[lands],
            send_sem=near_send.at[k],
            recv_sem=near_recv.at[lands],
            device_id=peer,
            device_id_type=MESH,
        )

    def each(first, last, act):
        def body(k, _):
            act(k)
            return 0

        lax.fori_loop(first, last, body, 0)

    each(0, 2 * n_s, lambda k: halo_copy(k, False).start())
    each(1, n_s, lambda k: sub_copy(k, False).start())
    each(1, slots, lambda k: coarse_copy(k, False).start())
    near_ref[n_s + s] = mult_ref[...]
    coarse_ref[mine] = pack[...]
    each(0, 2 * n_s, lambda k: halo_copy(k, True).wait_recv())
    each(1, n_s, lambda k: sub_copy(k, True).wait_recv())
    each(1, slots, lambda k: coarse_copy(k, True).wait_recv())
    each(0, 2 * n_s, lambda k: halo_copy(k, False).wait_send())
    each(1, n_s, lambda k: sub_copy(k, False).wait_send())
    each(1, slots, lambda k: coarse_copy(k, False).wait_send())


def one_hot(rows, height):
    ids = lax.broadcasted_iota(jnp.int32, (height, rows.shape[1]), 0).astype(F32)
    return jnp.where(ids == rows, 1.0, 0.0).astype(BF16)


def column_of(row, height):
    width = row.shape[1]
    at = lax.broadcasted_iota(jnp.int32, (height, width), 0)
    on = lax.broadcasted_iota(jnp.int32, (height, width), 1)
    return jnp.sum(jnp.where(at == on, row, 0.0), axis=1, keepdims=True)


def folded(values, per_row):
    n, cap = values.shape
    lanes = per_row * cap
    j = lax.broadcasted_iota(jnp.int32, (cap, lanes), 0)
    lane = lax.broadcasted_iota(jnp.int32, (cap, lanes), 1)
    spread = jnp.where(lane % cap == j, 1.0, 0.0).astype(BF16)
    wide = dot(values.astype(BF16), spread)
    at = lax.broadcasted_iota(jnp.int32, (n, lanes), 0)
    on = lax.broadcasted_iota(jnp.int32, (n, lanes), 1)
    wide = jnp.where(at % per_row == on // cap, wide, 0.0).astype(BF16)
    out = lax.broadcasted_iota(jnp.int32, (n // per_row, n), 0)
    src = lax.broadcasted_iota(jnp.int32, (n // per_row, n), 1)
    return dot(jnp.where(src // per_row == out, 1.0, 0.0).astype(BF16), wide)


def translate_kernel(
    n_m, near_ref, coarse_ref, tr_ref, t6_ref, s6_ref, c6_ref, t5_ref, s5_ref, c5_ref,
    t4_ref, s4_ref, c4_ref, out_ref, mats, mt, c5t, c4t, tg6, sr6, bl6, tg5, sr5, tg4, sr4,
    gather, total, sem,
):
    n_ops, width = tr_ref.shape[0], tr_ref.shape[2]
    padded = mats.shape[0]
    boxes = near_ref.shape[0] * near_ref.shape[1] // 3
    fives, fours = boxes // 8, boxes // 64
    cap6, cap5, cap4 = t6_ref.shape[2], t5_ref.shape[2], t4_ref.shape[2]
    copy = pltpu.make_async_copy(tr_ref, mats.at[pl.ds(0, n_ops)], sem)
    copy.start()
    for o in range(n_ops, padded):
        mats[o] = jnp.zeros(mats.shape[1:], BF16)

    m = lax.axis_index("morton")
    r = lax.broadcasted_iota(jnp.int32, (width, width), 0)
    c = lax.broadcasted_iota(jnp.int32, (width, width), 1)
    eye = jnp.where(r == c, 1.0, 0.0).astype(BF16)
    near = near_ref[...].reshape(3, boxes, width)
    for block in range(3):
        rows = dot_nt(eye, near[block])
        if block == 0:
            rows = jnp.where(m == 0, 0.0, rows)
        if block == 2:
            rows = jnp.where(m == n_m - 1, 0.0, rows)
        mt[pl.ds(block * width, width), :] = rows.astype(BF16)
    slots = coarse_ref.shape[0]
    packed = dot_nt(eye, coarse_ref[...].reshape(slots * PACK, width)).astype(BF16)
    q = lax.broadcasted_iota(jnp.int32, (slots * PACK, slots * 8), 0)
    p = lax.broadcasted_iota(jnp.int32, (slots * PACK, slots * 8), 1)
    c5t[...] = dot(packed, jnp.where(q == p // 8 * PACK + p % 8, 1.0, 0.0).astype(BF16)).astype(BF16)
    q = lax.broadcasted_iota(jnp.int32, (slots * PACK, slots), 0)
    p = lax.broadcasted_iota(jnp.int32, (slots * PACK, slots), 1)
    c4t[...] = dot(packed, jnp.where(q == p * PACK + 8, 1.0, 0.0).astype(BF16)).astype(BF16)

    def table(t_ref, c_ref, shift):
        cap = t_ref.shape[2]
        live = lax.broadcasted_iota(jnp.int32, (n_ops, cap), 1).astype(F32)
        live = live < column_of(c_ref[...].astype(F32), n_ops)
        return jnp.where(live, t_ref[0].astype(F32) + shift, shift - 1.0)

    def filled(values, fill):
        if padded == n_ops:
            return values
        more = jnp.full((padded - n_ops, values.shape[1]), fill, F32)
        return jnp.concatenate([values, more], axis=0)

    tg6[...] = filled(table(t6_ref, c6_ref, 0.0), -1.0)
    source = s6_ref[0]
    block = jnp.where(source >= boxes, 1, 0) + jnp.where(source >= 2 * boxes, 1, 0)
    sr6[...] = filled((source - block * boxes).astype(F32), 0.0)
    bl6[...] = filled(block.astype(F32), 0.0)

    def keys(t_ref, c_ref, per_row, height):
        raw = folded(filled(table(t_ref, c_ref, 1.0), 0.0), per_row)
        lane = lax.broadcasted_iota(jnp.int32, raw.shape, 1) // t_ref.shape[2]
        return jnp.where(raw > 0.0, raw - 1.0 + (lane * height).astype(F32), -1.0)

    tg5[...] = keys(t5_ref, c5_ref, 8, fives)
    sr5[...] = folded(filled(s5_ref[0].astype(F32), 0.0), 8)
    tg4[...] = keys(t4_ref, c4_ref, STEP, PACK)
    sr4[...] = folded(filled(s4_ref[0].astype(F32), 0.0), STEP)
    copy.wait()

    total[...] = jnp.zeros(total.shape, F32)
    zero = jnp.zeros((width, cap6), BF16)

    @pl.loop(0, padded // STEP)
    def _(step):
        for pair in range(STEP // 2):
            heads, places, picks = [], [], []
            for half in range(2):
                o = step * STEP + 2 * pair + half
                picks.append(one_hot(sr6[pl.ds(o, 1), :], boxes))
                places.append(one_hot(tg6[pl.ds(o, 1), :], boxes))
                heads.append(bl6[pl.ds(o, 1), :])
            found = dot(mt[...], jnp.concatenate(picks, axis=1))
            head = jnp.concatenate(heads, axis=1)
            found = jnp.where(
                head == 0.0,
                found[:width],
                jnp.where(head == 1.0, found[width : 2 * width], found[2 * width :]),
            ).astype(BF16)
            apart = jnp.concatenate(
                [
                    jnp.concatenate([found[:, :cap6], zero], axis=1),
                    jnp.concatenate([zero, found[:, cap6:]], axis=1),
                ],
                axis=0,
            )
            placed = dot_nt(jnp.concatenate(places, axis=1), apart)
            gather[pl.ds(0, boxes), pl.ds(pair * 2 * width, 2 * width)] = placed.astype(BF16)
        for half in range(STEP // 8):
            row = step * (STEP // 8) + half
            found = dot(c5t[...], one_hot(sr5[pl.ds(row, 1), :], c5t.shape[1])).astype(BF16)
            placed = dot_nt(one_hot(tg5[pl.ds(row, 1), :], 8 * fives), found).astype(BF16)
            for o in range(8):
                gather[pl.ds(boxes, fives), pl.ds((half * 8 + o) * width, width)] = placed[
                    o * fives : (o + 1) * fives
                ]
        found = dot(c4t[...], one_hot(sr4[pl.ds(step, 1), :], c4t.shape[1])).astype(BF16)
        placed = dot_nt(one_hot(tg4[pl.ds(step, 1), :], STEP * PACK), found).astype(BF16)
        for o in range(STEP):
            gather[pl.ds(boxes + fives, PACK), pl.ds(o * width, width)] = placed[
                o * PACK : (o + 1) * PACK
            ]
        ops = mats[pl.ds(step * STEP, STEP)].reshape(STEP * width, width)
        total[...] += dot(gather[...], ops)

    parts = out_ref.shape[0]
    six, five, four = boxes // parts, fives // parts, fours // parts
    for part in range(parts):
        out_ref[part, pl.ds(0, six), :] = total[pl.ds(part * six, six), :].astype(BF16)
        tail = jnp.concatenate(
            [
                total[pl.ds(boxes + part * five, five), :] * 0.5,
                total[pl.ds(boxes + fives + part * four, four), :] * 0.25,
                jnp.zeros((PACK - five - four, width), F32),
            ],
            axis=0,
        )
        out_ref[part, pl.ds(six, PACK), :] = tail.astype(BF16)


def combine_kernel(sizes, part_ref, down_ref, out_ref, got, wide, send, recv):
    n_m, n_s = sizes
    m, s = lax.axis_index("morton"), lax.axis_index("sub")
    barrier = pltpu.get_barrier_semaphore()
    for k in range(1, n_s):
        pl.semaphore_signal(barrier, inc=1, device_id=(m, (s + k) % n_s), device_id_type=MESH)
    pl.semaphore_wait(barrier, n_s - 1)

    def part_copy(k):
        other = (s + k) % n_s
        return pltpu.make_async_remote_copy(
            src_ref=part_ref.at[other],
            dst_ref=got.at[k],
            send_sem=send.at[k],
            recv_sem=recv.at[k],
            device_id=(m, other),
            device_id_type=MESH,
        )

    for k in range(1, n_s):
        part_copy(k).start()
    total = part_ref[s].astype(F32)
    for k in range(1, n_s):
        part_copy(k).wait_recv()
        total = total + got[k].astype(F32)
    six = out_ref.shape[0]
    four = total[six + 8 : six + 9, :].astype(BF16)
    spread = [dot(four, down_ref[c]) for c in range(8)]
    five = (total[six : six + 8, :] + jnp.concatenate(spread, axis=0)).astype(BF16)
    for c in range(8):
        wide[pl.ds(c, six // 8, stride=8), :] = dot(five, down_ref[c])
    out_ref[...] = (wide[...] + total[:six, :]).astype(BF16)
    for k in range(1, n_s):
        part_copy(k).wait_send()


VMEM = pl.BlockSpec(memory_space=pltpu.VMEM)


def local(sizes, mult, trans, up, down, t6, s6, c6, t5, s5, c5, t4, s4, c4):
    n_m, n_s = sizes
    quarter, width = mult.shape
    boxes = quarter * n_s
    slots = GROUP * n_s
    near, coarse = pl.pallas_call(
        functools.partial(exchange_kernel, sizes),
        out_shape=(
            jax.ShapeDtypeStruct((3 * n_s, quarter, width), BF16),
            jax.ShapeDtypeStruct((slots, PACK, width), BF16),
        ),
        in_specs=[VMEM] * 2,
        out_specs=(VMEM, VMEM),
        scratch_shapes=[
            pltpu.VMEM((quarter, width), F32),
            pltpu.VMEM((PACK, width), BF16),
            pltpu.SemaphoreType.DMA((3 * n_s,)),
            pltpu.SemaphoreType.DMA((3 * n_s,)),
            pltpu.SemaphoreType.DMA((slots,)),
            pltpu.SemaphoreType.DMA((slots,)),
        ],
        compiler_params=pltpu.CompilerParams(collective_id=0, has_side_effects=True),
        name="exchange",
    )(mult, up)

    n_ops = trans.shape[0]
    padded = -(-n_ops // STEP) * STEP
    rows = boxes + boxes // 8 + PACK
    parts = pl.pallas_call(
        functools.partial(translate_kernel, n_m),
        out_shape=jax.ShapeDtypeStruct((n_s, quarter + PACK, width), BF16),
        in_specs=[VMEM, VMEM, pl.BlockSpec(memory_space=pl.ANY)] + [VMEM] * 9,
        out_specs=VMEM,
        scratch_shapes=[
            pltpu.VMEM((padded, width, width), BF16),
            pltpu.VMEM((3 * width, boxes), BF16),
            pltpu.VMEM((width, slots * 8), BF16),
            pltpu.VMEM((width, slots), BF16),
            pltpu.VMEM((padded, t6.shape[2]), F32),
            pltpu.VMEM((padded, t6.shape[2]), F32),
            pltpu.VMEM((padded, t6.shape[2]), F32),
            pltpu.VMEM((padded // 8, 8 * t5.shape[2]), F32),
            pltpu.VMEM((padded // 8, 8 * t5.shape[2]), F32),
            pltpu.VMEM((padded // STEP, STEP * t4.shape[2]), F32),
            pltpu.VMEM((padded // STEP, STEP * t4.shape[2]), F32),
            pltpu.VMEM((rows, STEP * width), BF16),
            pltpu.VMEM((rows, width), F32),
            pltpu.SemaphoreType.DMA,
        ],
        compiler_params=pltpu.CompilerParams(vmem_limit_bytes=32 * 1024 * 1024),
        name="translate",
    )(near, coarse, trans, t6, s6, c6, t5, s5, c5, t4, s4, c4)

    return pl.pallas_call(
        functools.partial(combine_kernel, sizes),
        out_shape=jax.ShapeDtypeStruct((quarter, width), BF16),
        in_specs=[VMEM] * 2,
        out_specs=VMEM,
        scratch_shapes=[
            pltpu.VMEM((n_s, quarter + PACK, width), BF16),
            pltpu.VMEM((quarter, width), F32),
            pltpu.SemaphoreType.DMA((n_s,)),
            pltpu.SemaphoreType.DMA((n_s,)),
        ],
        compiler_params=pltpu.CompilerParams(collective_id=1, has_side_effects=True),
        name="combine",
    )(parts, down)


def solution(mesh):
    sizes = (mesh.shape["morton"], mesh.shape["sub"])
    placed = (
        P(("morton", "sub"), None),
        P("sub", None, None),
        P(),
        P(),
        P("morton", "sub", None),
        P("morton", "sub", None),
        P("morton", "sub"),
        P("morton", "sub", None),
        P("morton", "sub", None),
        P("morton", "sub"),
        P("morton", "sub", None),
        P("morton", "sub", None),
        P("morton", "sub"),
    )
    return jax.shard_map(
        functools.partial(local, sizes),
        mesh=mesh,
        in_specs=placed,
        out_specs=P(("morton", "sub"), None),
        check_vma=False,
    )
```

time: 100 us -> 51.7 us (0.52)
  Pallas kernels: 0 us -> 38.9 us
  matrix products: 29.9 us -> 0 us
  blocking collectives: 27.1 us -> 0 us
  between operations: 14.3 us -> 0.05 us
  starting transfers between devices: 13.4 us -> 0 us
  other arithmetic: 6.15 us -> 0 us
  local copies, waits for them, and re-layouts: 8.67 us -> 12.2 us
    pallas_call x0 -> x3, Pallas kernels: none -> 38.9 us  [the longest x1 17.2 us: local(): pl.pallas_call(functools.partial(translate_kernel, n_m), out_shape=jax.Sh...]
    dot_general x13 -> x0, matrix products: 29.9 us -> none  [the longest x3 14 us: single_rotation(): jnp.einsum('kt,kc->tc', placing, product.reshape(-1, coeff_width), precis...]
    all_gather x3 -> x0, blocking collectives: 15.8 us -> none  [the longest x1 5.59 us: local(): nearby = lax.all_gather(with_rims, 'sub', axis=0, tiled=True)]
    ppermute x5 -> x0, starting transfers between devices: 13.4 us -> none  [the longest x3 7 us: swapped(): lax.ppermute(shard, axis, [(i, i ^ 1 << apart) for i in range(lax.axis_si...]
    unnamed x1 -> x0, blocking collectives: 11.3 us -> none
    unnamed x10 -> x21, local copies, waits for them, and re-layouts: 4.45 us -> 12.2 us
    reshape x2 -> x0, local copies, waits for them, and re-layouts: 2.39 us -> none  [the longest x1 1.57 us: single_rotation(): product.reshape(-1, coeff_width)]
    lt x3 -> x0, other arithmetic: 2.2 us -> none  [single_rotation(): is_live = (slot_numbers[None, :] < counts[:, None]).reshape(-1)]
  transfers between devices with their start and end apart: 6 -> 0, of which waited for: 0 -> 0; matrix products, arithmetic and copies ran while one was open for 44% -> 0% of each run, Pallas kernels for 0% -> 0%
where the time goes in v1:
time: 51.7 us; the launch traced here: 51.2 us
  Pallas kernels  38.9 us (75%)
  local copies, waits for them, and re-layouts  12.2 us (24%)
    pallas_call x1, Pallas kernels, local(): pl.pallas_call(functools.partial(translate_kernel, n_m), out_shape=jax.Sh...  17.2 us
    pallas_call x1, Pallas kernels, local(): pl.pallas_call(functools.partial(exchange_kernel, sizes), out_shape=(jax....  16 us
    unnamed x21, local copies, waits for them, and re-layouts  12.2 us
    pallas_call x1, Pallas kernels, local(): pl.pallas_call(functools.partial(combine_kernel, sizes), out_shape=jax.Sh...  5.81 us

profile of v1, /device:TPU:0, one launch (start us, length us, event | category | flops | bytes accessed | tf_op | source)
XLA Modules:
  0.0 51.2 jit_solution(13753429124639392859)
XLA Ops:
  0.0 0.8 %copy.14.t6_ref = s32[1,79,128]{2,1,0:T(8,128)S(1)} copy(s32[1,79,128]{2,0,1:T(1,128)} %param.17) | data formatting | bytes 80896 | tf_op args[4]
  0.8 0.8 %copy.15.s6_ref = s32[1,79,128]{2,1,0:T(8,128)S(1)} copy(s32[1,79,128]{2,0,1:T(1,128)} %param.18) | data formatting | bytes 80896 | tf_op args[5]
  1.6 0.8 %copy.16.t5_ref = s32[1,79,16]{2,1,0:T(8,128)S(1)} copy(s32[1,79,16]{1,2,0:T(8,128)} %param.20) | data formatting | bytes 10112 | tf_op args[7]
  2.4 0.8 %copy.17.s5_ref = s32[1,79,16]{2,1,0:T(8,128)S(1)} copy(s32[1,79,16]{1,2,0:T(8,128)} %param.21) | data formatting | bytes 10112 | tf_op args[8]
  3.2 0.8 %copy.18.t4_ref = s32[1,79,2]{2,1,0:T(8,128)S(1)} copy(s32[1,79,2]{1,2,0:T(2,128)} %param.23) | data formatting | bytes 1264 | tf_op args[10]
  3.9 0.8 %copy.19.s4_ref = s32[1,79,2]{2,1,0:T(8,128)S(1)} copy(s32[1,79,2]{1,2,0:T(2,128)} %param.24) | data formatting | bytes 1264 | tf_op args[11]
  4.7 16.0 %exchange.1 = (bf16[12,64,128]{2,1,0:T(8,128)(2,1)}, bf16[32,16,128]{2,1,0:T(8,128)(2,1)}) custom-call(bf16[64,128]{1,0:T(8,128)(2,1)} %mult_ref.1, bf16[8,128,128]{2,1,0:T(8,128)(2,1)} %up_ref.1), custom_call_target="tpu_custom_call" | custom-call | tf_op jit(solution)/shard_map/exchange/pallas_call | solution.py:333
  20.7 0.0 copy-start
  20.7 1.7 %copy-done = bf16[79,128,128]{2,1,0:T(8,128)(2,1)S(1)} copy-done((bf16[79,128,128]{2,1,0:T(8,128)(2,1)S(1)}, bf16[79,128,128]{2,1,0:T(8,128)(2,1)}, u32[]{:S(2)}) %copy-start) | copy-done | bytes 2588696
  22.4 0.0 copy-start.2
  22.4 0.9 %copy-done.2 = bf16[12,64,128]{2,1,0:T(8,128)(2,1)S(1)} copy-done((bf16[12,64,128]{2,1,0:T(8,128)(2,1)S(1)}, bf16[12,64,128]{2,1,0:T(8,128)(2,1)}, u32[]{:S(2)}) %copy-start.2) | copy-done | bytes 196632
  23.4 0.0 copy-start.3
  23.4 0.9 %copy-done.3 = bf16[32,16,128]{2,1,0:T(8,128)(2,1)S(1)} copy-done((bf16[32,16,128]{2,1,0:T(8,128)(2,1)S(1)}, bf16[32,16,128]{2,1,0:T(8,128)(2,1)}, u32[]{:S(2)}) %copy-start.3) | copy-done | bytes 131096
  24.3 0.0 copy-start.4
  24.3 0.7 %copy-done.4 = s32[1,79]{1,0:T(1,128)S(1)} copy-done((s32[1,79]{1,0:T(1,128)S(1)}, s32[1,79]{1,0:T(1,128)}, u32[]{:S(2)}) %copy-start.4) | copy-done | bytes 340
  24.9 0.0 copy-start.5
  24.9 0.7 %copy-done.5 = s32[1,79]{1,0:T(1,128)S(1)} copy-done((s32[1,79]{1,0:T(1,128)S(1)}, s32[1,79]{1,0:T(1,128)}, u32[]{:S(2)}) %copy-start.5) | copy-done | bytes 340
  25.6 0.0 copy-start.6
  25.6 0.7 %copy-done.6 = s32[1,79]{1,0:T(1,128)S(1)} copy-done((s32[1,79]{1,0:T(1,128)S(1)}, s32[1,79]{1,0:T(1,128)}, u32[]{:S(2)}) %copy-start.6) | copy-done | bytes 340
  26.2 17.2 %translate.1.part_ref = bf16[4,80,128]{2,1,0:T(8,128)(2,1)S(1)} custom-call(bf16[12,64,128]{2,1,0:T(8,128)(2,1)S(1)} %copy-done.2, bf16[32,16,128]{2,1,0:T(8,128)(2,1)S(1)} %copy-done.3, bf16[79,128,128]{2,1,0:T(8,128)(2,1)S(1)} %copy-done, s32[1,79,128]{2,1,0:T(8,128)S(1)} %copy.14.t6_ref, s32[1,79,128]{2,1,0:T(8,128)S(1)} %copy.15.s6_ref, ...), custom_call_target="tpu_custom_call" | custom-call | tf_op jit(solution)/shard_map/translate/pallas_call | solution.py:356
  43.4 0.0 copy-start.1
  43.4 0.6 %copy-done.1 = bf16[4,80,128]{2,1,0:T(8,128)(2,1)} copy-done((bf16[4,80,128]{2,1,0:T(8,128)(2,1)}, bf16[4,80,128]{2,1,0:T(8,128)(2,1)S(1)}, u32[]{:S(2)}) %copy-start.1) | copy-done | bytes 81944
  44.0 5.8 %combine.1 = bf16[64,128]{1,0:T(8,128)(2,1)} custom-call(bf16[4,80,128]{2,1,0:T(8,128)(2,1)} %copy-done.1, bf16[8,128,128]{2,1,0:T(8,128)(2,1)} %down_ref.1), custom_call_target="tpu_custom_call" | custom-call | tf_op jit(solution)/shard_map/combine/pallas_call | solution.py:381
  49.9 1.3 %copy.21 = bf16[64,128]{1,0:T(8,128)(2,1)} copy(bf16[64,128]{1,0:T(8,128)(2,1)} %combine.1) | data formatting | bytes 32768
Async XLA Ops:
  20.7 1.7 %copy-start = (bf16[79,128,128]{2,1,0:T(8,128)(2,1)S(1)}, bf16[79,128,128]{2,1,0:T(8,128)(2,1)}, u32[]{:S(2)}) copy-start(bf16[79,128,128]{2,1,0:T(8,128)(2,1)} %tr_ref.1) | copy-start | bytes 7766020
  22.4 0.9 %copy-start.2 = (bf16[12,64,128]{2,1,0:T(8,128)(2,1)S(1)}, bf16[12,64,128]{2,1,0:T(8,128)(2,1)}, u32[]{:S(2)}) copy-start(bf16[12,64,128]{2,1,0:T(8,128)(2,1)} %get-tuple-element.7.near_ref) | copy-start | bytes 589828
  23.4 0.9 %copy-start.3 = (bf16[32,16,128]{2,1,0:T(8,128)(2,1)S(1)}, bf16[32,16,128]{2,1,0:T(8,128)(2,1)}, u32[]{:S(2)}) copy-start(bf16[32,16,128]{2,1,0:T(8,128)(2,1)} %get-tuple-element.8.coarse_ref) | copy-start | bytes 393220
  24.3 0.7 %copy-start.4 = (s32[1,79]{1,0:T(1,128)S(1)}, s32[1,79]{1,0:T(1,128)}, u32[]{:S(2)}) copy-start(s32[1,79]{1,0:T(1,128)} %c6_ref.1) | copy-start | bytes 952
  24.9 0.7 %copy-start.5 = (s32[1,79]{1,0:T(1,128)S(1)}, s32[1,79]{1,0:T(1,128)}, u32[]{:S(2)}) copy-start(s32[1,79]{1,0:T(1,128)} %c5_ref.1) | copy-start | bytes 952
  25.6 0.7 %copy-start.6 = (s32[1,79]{1,0:T(1,128)S(1)}, s32[1,79]{1,0:T(1,128)}, u32[]{:S(2)}) copy-start(s32[1,79]{1,0:T(1,128)} %c4_ref.1) | copy-start | bytes 952
  43.4 0.6 %copy-start.1 = (bf16[4,80,128]{2,1,0:T(8,128)(2,1)}, bf16[4,80,128]{2,1,0:T(8,128)(2,1)S(1)}, u32[]{:S(2)}) copy-start(bf16[4,80,128]{2,1,0:T(8,128)(2,1)S(1)} %translate.1.part_ref) | copy-start | bytes 245764

commit v2 on v0

v2 whole, which is shorter than its diff:
```python
import functools

import jax
import jax.numpy as jnp
from jax import lax
from jax.experimental import pallas as pl
from jax.experimental.pallas import tpu as pltpu
from jax.sharding import PartitionSpec as P

BF16 = jnp.bfloat16
F32 = jnp.float32
MESH = pl.DeviceIdType.MESH
GROUP = 8
PACK = 16
STEP = 16


def dot(a, b):
    return jnp.dot(a, b, preferred_element_type=F32)


def dot_nt(a, b):
    return lax.dot_general(a, b, (((1,), (1,)), ((), ())), preferred_element_type=F32)


def column_of(row, height):
    width = row.shape[1]
    at = lax.broadcasted_iota(jnp.int32, (height, width), 0)
    on = lax.broadcasted_iota(jnp.int32, (height, width), 1)
    return jnp.sum(jnp.where(at == on, row, 0.0), axis=1, keepdims=True)


def folded(values, per_row):
    n, cap = values.shape
    lanes = per_row * cap
    j = lax.broadcasted_iota(jnp.int32, (cap, lanes), 0)
    lane = lax.broadcasted_iota(jnp.int32, (cap, lanes), 1)
    spread = jnp.where(lane % cap == j, 1.0, 0.0).astype(BF16)
    wide = dot(values.astype(BF16), spread)
    at = lax.broadcasted_iota(jnp.int32, (n, lanes), 0)
    on = lax.broadcasted_iota(jnp.int32, (n, lanes), 1)
    wide = jnp.where(at % per_row == on // cap, wide, 0.0).astype(BF16)
    out = lax.broadcasted_iota(jnp.int32, (n // per_row, n), 0)
    src = lax.broadcasted_iota(jnp.int32, (n // per_row, n), 1)
    return dot(jnp.where(src // per_row == out, 1.0, 0.0).astype(BF16), wide)


def one_hot(ids, row):
    height, lanes = ids.shape
    rows = jnp.broadcast_to(row, (16, lanes)).astype(BF16)
    same = ids.reshape(height // 16, 16, lanes) == rows[None]
    one, none = jnp.ones((), BF16), jnp.zeros((), BF16)
    return jnp.where(same, one, none).reshape(height, lanes)


def wrapped(value, size):
    return jnp.where(value >= size, value - size, value)


def upward_rows(children, up, wide):
    parents = children.shape[0] // 8
    wide[...] = children.astype(F32)
    rows = [wide[pl.ds(c, parents, stride=8), :] for c in range(8)]
    ops = up.reshape(-1, up.shape[2])
    five = dot(jnp.concatenate(rows, axis=1).astype(BF16), ops).astype(BF16).astype(F32)
    row = jnp.concatenate([five[c : c + 1, :] for c in range(8)], axis=1).astype(BF16)
    pad = jnp.zeros((PACK - parents - 1, five.shape[1]), F32)
    return jnp.concatenate([five, dot(row, ops), pad], axis=0).astype(BF16)


def kernel(
    sizes, mult_hbm, tr_hbm, up_hbm, down_hbm, t6_hbm, s6_hbm, c6_hbm, t5_hbm, s5_hbm, c5_hbm,
    t4_hbm, s4_hbm, c4_hbm, out_ref,
    near, coarse, mats, up, down, t6, s6, c6, t5, s5, c5, t4, s4, c4,
    wide, mt, c5t, c4t, tg6, sr6, bl6, tg5, sr5, tg4, sr4,
    picks, places, apart, gather, parts, got,
    load, near_send, near_recv, pass_send, pack_send, pack_recv, join_send, join_recv,
    part_send, part_recv,
):
    n_m, n_s = sizes
    n_ops, width = tr_hbm.shape[0], tr_hbm.shape[2]
    padded = mats.shape[0]
    quarter = near.shape[1]
    boxes = quarter * n_s
    fives, fours = boxes // 8, boxes // 64
    cap6, cap5, cap4 = t6.shape[2], t5.shape[1], t4.shape[1]
    m, s = lax.axis_index("morton"), lax.axis_index("sub")
    base = m * 0 if n_m == GROUP else m // GROUP * GROUP
    here = m - base
    following = wrapped(m + 1, n_m)
    previous = jnp.where(m == 0, n_m - 1, m - 1)

    barrier = pltpu.get_barrier_semaphore()

    def greet(peer):
        pl.semaphore_signal(barrier, inc=1, device_id=peer, device_id_type=MESH)

    for k in range(1, n_s):
        greet((m, wrapped(s + k, n_s)))
    for k in range(1, GROUP):
        greet((base + wrapped(here + k, GROUP), s))
    expected = n_s - 1 + GROUP - 1
    if n_m > GROUP:
        greet((following, s))
        greet((previous, s))
        expected = expected + 2

    own = near.at[n_s + s]
    pairs = [
        (mult_hbm, own), (up_hbm, up), (c6_hbm, c6), (t6_hbm, t6), (s6_hbm, s6),
        (c5_hbm, c5), (t5_hbm, t5), (s5_hbm, s5), (c4_hbm, c4), (t4_hbm, t4), (s4_hbm, s4),
        (tr_hbm, mats.at[pl.ds(0, n_ops)]), (down_hbm, down),
    ]
    loads = [pltpu.make_async_copy(a, b, load.at[i]) for i, (a, b) in enumerate(pairs)]
    for copy in loads:
        copy.start()

    def remote(src, dst, send, recv, peer):
        return pltpu.make_async_remote_copy(
            src_ref=src, dst_ref=dst, send_sem=send, recv_sem=recv,
            device_id=peer, device_id_type=MESH,
        )

    def halo_copy(side):
        slot = side * 2 * n_s + s
        return remote(
            own, near.at[slot], near_send.at[side], near_recv.at[slot],
            (previous if side else following, s),
        )

    def sub_copy(k, there):
        other = wrapped(s + k, n_s)
        slot = n_s + (other if there else s)
        return remote(
            own, near.at[slot], near_send.at[2 + k], near_recv.at[slot], (m, other)
        )

    def pass_copy(side, k, there):
        other = wrapped(s + k, n_s)
        slot = side * 2 * n_s + (other if there else s)
        return remote(
            near.at[slot], near.at[slot], pass_send.at[side * n_s + k], near_recv.at[slot],
            (m, other),
        )

    def pack_copy(k, there):
        other = wrapped(s + k, n_s)
        slot = coarse.at[here, other if there else s]
        return remote(
            slot, slot, pack_send.at[k], pack_recv.at[other if there else s], (m, other)
        )

    def join_copy(k, there):
        other = wrapped(here + k, GROUP)
        slot = other if there else here
        return remote(
            coarse.at[slot], coarse.at[slot], join_send.at[k], join_recv.at[slot],
            (base + other, s),
        )

    def part_copy(k):
        other = wrapped(s + k, n_s)
        return remote(
            parts.at[other], got.at[k], part_send.at[k], part_recv.at[k], (m, other)
        )

    loads[0].wait()
    pl.semaphore_wait(barrier, expected)
    for side in range(2):
        halo_copy(side).start()
    for k in range(1, n_s):
        sub_copy(k, False).start()
    loads[1].wait()
    coarse[here, s] = upward_rows(near[n_s + s], up[...], wide)
    for k in range(1, n_s):
        pack_copy(k, False).start()

    for copy in loads[2:11]:
        copy.wait()

    def filled(values, fill):
        if padded == n_ops:
            return values
        more = jnp.full((padded - n_ops, values.shape[1]), fill, F32)
        return jnp.concatenate([values, more], axis=0)

    lane = lax.broadcasted_iota(jnp.int32, (n_ops, cap6), 1).astype(F32)
    live = lane < column_of(c6[...].astype(F32), n_ops)
    tg6[...] = filled(jnp.where(live, t6[:, 0, :].astype(F32), -1.0), -1.0)
    source = s6[:, 0, :]
    block = jnp.where(source >= boxes, 1, 0) + jnp.where(source >= 2 * boxes, 1, 0)
    sr6[...] = filled((source - block * boxes).astype(F32), 0.0)
    bl6[...] = filled(block.astype(F32), 0.0)

    at = lax.broadcasted_iota(jnp.int32, (padded, n_ops), 0)
    on = lax.broadcasted_iota(jnp.int32, (padded, n_ops), 1)
    turn = jnp.where(at == on, 1.0, 0.0).astype(BF16)

    def keys(t_ref, c_ref, per_row, height):
        cap = t_ref.shape[1]
        slot = lax.broadcasted_iota(jnp.int32, (cap, n_ops), 0)
        alive = jnp.where(slot < c_ref[...], t_ref[0] + 1, 0).astype(F32).astype(BF16)
        raw = folded(dot_nt(turn, alive), per_row)
        lane = lax.broadcasted_iota(jnp.int32, raw.shape, 1) // cap
        return jnp.where(raw > 0.0, raw - 1.0 + (lane * height).astype(F32), -1.0)

    def sources(s_ref, per_row):
        return folded(dot_nt(turn, s_ref[0].astype(F32).astype(BF16)), per_row)

    tg5[...] = keys(t5, c5, 8, fives)
    sr5[...] = sources(s5, 8)
    tg4[...] = keys(t4, c4, STEP, PACK)
    sr4[...] = sources(s4, STEP)
    for o in range(n_ops, padded):
        mats[o] = jnp.zeros(mats.shape[1:], BF16)
    apart[...] = jnp.zeros(apart.shape, BF16)

    for side in range(2):
        halo_copy(side).wait_recv()
        for k in range(1, n_s):
            pass_copy(side, k, False).start()
    for k in range(1, n_s):
        pack_copy(k, True).wait_recv()
    for k in range(1, GROUP):
        join_copy(k, False).start()
    for k in range(1, n_s):
        sub_copy(k, True).wait_recv()
    for side in range(2):
        for k in range(1, n_s):
            pass_copy(side, k, True).wait_recv()

    r = lax.broadcasted_iota(jnp.int32, (width, width), 0)
    c = lax.broadcasted_iota(jnp.int32, (width, width), 1)
    eye = jnp.where(r == c, 1.0, 0.0).astype(BF16)
    nearby = near[...].reshape(3, boxes, width)
    for block in range(3):
        rows = dot_nt(eye, nearby[block])
        if block == 0:
            rows = jnp.where(m == 0, 0.0, rows)
        if block == 2:
            rows = jnp.where(m == n_m - 1, 0.0, rows)
        mt[pl.ds(block * width, width), :] = rows.astype(BF16)

    ids = lax.broadcasted_iota(jnp.int32, (boxes, cap6), 0).astype(F32).astype(BF16)

    @pl.loop(0, padded // STEP)
    def _(step):
        def mark(pair):
            for half in range(2):
                o = step * STEP + 2 * pair + half
                lanes = pl.ds((2 * pair + half) * cap6, cap6)
                picks[:, lanes] = one_hot(ids, sr6[pl.ds(o, 1), :])
                places[:, lanes] = one_hot(ids, tg6[pl.ds(o, 1), :])

        def pick(pair):
            found = dot(mt[...], picks[:, pl.ds(2 * pair * cap6, 2 * cap6)])
            for half in range(2):
                head = bl6[pl.ds(step * STEP + 2 * pair + half, 1), :]
                piece = found[:, half * cap6 : (half + 1) * cap6]
                apart[pair, pl.ds(half * width, width), pl.ds(half * cap6, cap6)] = jnp.where(
                    head == 0.0,
                    piece[:width],
                    jnp.where(head == 1.0, piece[width : 2 * width], piece[2 * width :]),
                ).astype(BF16)

        def place(pair):
            placed = dot_nt(places[:, pl.ds(2 * pair * cap6, 2 * cap6)], apart[pair])
            lanes = pl.ds(
                pl.multiple_of(step * STEP * width + 2 * pair * width, 2 * width), 2 * width
            )
            gather[pl.ds(0, boxes), lanes] = placed.astype(BF16)

        for turn in range(STEP // 2 + 2):
            if turn >= 2:
                place(turn - 2)
            if 1 <= turn <= STEP // 2:
                pick(turn - 1)
            if turn < STEP // 2:
                mark(turn)

    for k in range(1, GROUP):
        join_copy(k, True).wait_recv()
    slots = GROUP * n_s
    packed = dot_nt(eye, coarse[...].reshape(slots * PACK, width)).astype(BF16)
    q = lax.broadcasted_iota(jnp.int32, (slots * PACK, slots * 8), 0)
    p = lax.broadcasted_iota(jnp.int32, (slots * PACK, slots * 8), 1)
    c5t[...] = dot(packed, jnp.where(q == p // 8 * PACK + p % 8, 1.0, 0.0).astype(BF16)).astype(BF16)
    q = lax.broadcasted_iota(jnp.int32, (slots * PACK, slots), 0)
    p = lax.broadcasted_iota(jnp.int32, (slots * PACK, slots), 1)
    c4t[...] = dot(packed, jnp.where(q == p * PACK + 8, 1.0, 0.0).astype(BF16)).astype(BF16)

    def numbers(height, lanes):
        return lax.broadcasted_iota(jnp.int32, (height, lanes), 0).astype(F32).astype(BF16)

    source5, target5 = numbers(slots * 8, 8 * cap5), numbers(8 * fives, 8 * cap5)
    source4, target4 = numbers(slots, STEP * cap4), numbers(STEP * PACK, STEP * cap4)

    @pl.loop(0, padded // STEP)
    def _(step):
        def at(o):
            return pl.ds(pl.multiple_of(step * STEP * width + o * width, width), width)

        for half in range(STEP // 8):
            row = step * (STEP // 8) + half
            found = dot(c5t[...], one_hot(source5, sr5[pl.ds(row, 1), :])).astype(BF16)
            placed = dot_nt(one_hot(target5, tg5[pl.ds(row, 1), :]), found).astype(BF16)
            for o in range(8):
                gather[pl.ds(boxes, fives), at(half * 8 + o)] = placed[o * fives : (o + 1) * fives]
        found = dot(c4t[...], one_hot(source4, sr4[pl.ds(step, 1), :])).astype(BF16)
        placed = dot_nt(one_hot(target4, tg4[pl.ds(step, 1), :]), found).astype(BF16)
        for o in range(STEP):
            gather[pl.ds(boxes + fives, PACK), at(o)] = placed[o * PACK : (o + 1) * PACK]

    loads[11].wait()
    total = dot(gather[...], mats[...].reshape(padded * width, width))

    six, five, four = boxes // n_s, fives // n_s, fours // n_s
    for part in range(n_s):
        parts[part, pl.ds(0, six), :] = total[part * six : (part + 1) * six].astype(BF16)
        low = boxes + fives + part * four
        tail = jnp.concatenate(
            [
                total[boxes + part * five : boxes + (part + 1) * five] * 0.5,
                total[low : low + four] * 0.25,
                jnp.zeros((PACK - five - four, width), F32),
            ],
            axis=0,
        )
        parts[part, pl.ds(six, PACK), :] = tail.astype(BF16)
    for k in range(1, n_s):
        part_copy(k).start()
    loads[12].wait()
    whole = parts[s].astype(F32)
    for k in range(1, n_s):
        part_copy(k).wait_recv()
        whole = whole + got[k].astype(F32)
    row = whole[six + five : six + five + 1, :].astype(BF16)
    spread = [dot(row, down[c]) for c in range(8)]
    mid = (whole[six : six + five, :] + jnp.concatenate(spread, axis=0)).astype(BF16)
    for c in range(8):
        wide[pl.ds(c, six // 8, stride=8), :] = dot(mid, down[c])
    out_ref[...] = (wide[...] + whole[:six, :]).astype(BF16)

    for side in range(2):
        halo_copy(side).wait_send()
        for k in range(1, n_s):
            pass_copy(side, k, False).wait_send()
    for k in range(1, n_s):
        sub_copy(k, False).wait_send()
        pack_copy(k, False).wait_send()
        part_copy(k).wait_send()
    for k in range(1, GROUP):
        join_copy(k, False).wait_send()


def local(sizes, mult, trans, up, down, t6, s6, c6, t5, s5, c5, t4, s4, c4):
    n_m, n_s = sizes
    quarter, width = mult.shape
    boxes = quarter * n_s
    slots = GROUP * n_s
    n_ops = trans.shape[0]
    padded = -(-n_ops // STEP) * STEP
    rows = boxes + boxes // 8 + PACK
    cap6, cap5, cap4 = t6.shape[2], t5.shape[2], t4.shape[2]
    t6, s6 = jnp.swapaxes(t6, 0, 1), jnp.swapaxes(s6, 0, 1)
    t5, s5, t4, s4 = (jnp.swapaxes(x, 1, 2) for x in (t5, s5, t4, s4))
    index = [pltpu.VMEM(x.shape, x.dtype) for x in (t6, s6, c6, t5, s5, c5, t4, s4, c4)]
    sems = pltpu.SemaphoreType.DMA
    return pl.pallas_call(
        functools.partial(kernel, sizes),
        out_shape=jax.ShapeDtypeStruct((quarter, width), BF16),
        in_specs=[pl.BlockSpec(memory_space=pl.ANY)] * 13,
        out_specs=pl.BlockSpec(memory_space=pltpu.VMEM),
        scratch_shapes=[
            pltpu.VMEM((3 * n_s, quarter, width), BF16),
            pltpu.VMEM((GROUP, n_s, PACK, width), BF16),
            pltpu.VMEM((padded, width, width), BF16),
            pltpu.VMEM(up.shape, BF16),
            pltpu.VMEM(down.shape, BF16),
            *index,
            pltpu.VMEM((quarter, width), F32),
            pltpu.VMEM((3 * width, boxes), BF16),
            pltpu.VMEM((width, slots * 8), BF16),
            pltpu.VMEM((width, slots), BF16),
            pltpu.VMEM((padded, cap6), F32),
            pltpu.VMEM((padded, cap6), F32),
            pltpu.VMEM((padded, cap6), F32),
            pltpu.VMEM((padded // 8, 8 * cap5), F32),
            pltpu.VMEM((padded // 8, 8 * cap5), F32),
            pltpu.VMEM((padded // STEP, STEP * cap4), F32),
            pltpu.VMEM((padded // STEP, STEP * cap4), F32),
            pltpu.VMEM((boxes, STEP * cap6), BF16),
            pltpu.VMEM((boxes, STEP * cap6), BF16),
            pltpu.VMEM((STEP // 2, 2 * width, 2 * cap6), BF16),
            pltpu.VMEM((rows, padded * width), BF16),
            pltpu.VMEM((n_s, quarter + PACK, width), BF16),
            pltpu.VMEM((n_s, quarter + PACK, width), BF16),
            sems((13,)),
            sems((2 + n_s,)),
            sems((3 * n_s,)),
            sems((2 * n_s,)),
            sems((n_s,)),
            sems((n_s,)),
            sems((GROUP,)),
            sems((GROUP,)),
            sems((n_s,)),
            sems((n_s,)),
        ],
        compiler_params=pltpu.CompilerParams(
            collective_id=0, has_side_effects=True, vmem_limit_bytes=48 * 1024 * 1024
        ),
        name="far_field",
    )(mult, trans, up, down, t6, s6, c6, t5, s5, c5, t4, s4, c4)


def solution(mesh):
    sizes = (mesh.shape["morton"], mesh.shape["sub"])
    placed = (
        P(("morton", "sub"), None),
        P("sub", None, None),
        P(),
        P(),
        P("morton", "sub", None),
        P("morton", "sub", None),
        P("morton", "sub"),
        P("morton", "sub", None),
        P("morton", "sub", None),
        P("morton", "sub"),
        P("morton", "sub", None),
        P("morton", "sub", None),
        P("morton", "sub"),
    )
    return jax.shard_map(
        functools.partial(local, sizes),
        mesh=mesh,
        in_specs=placed,
        out_specs=P(("morton", "sub"), None),
        check_vma=False,
    )
```

time: 100 us -> 46 us (0.46)
  Pallas kernels: 0 us -> 34.2 us
  matrix products: 29.9 us -> 0 us
  blocking collectives: 27.1 us -> 0 us
  between operations: 14.3 us -> 0.02 us
  starting transfers between devices: 13.4 us -> 0 us
  other arithmetic: 6.15 us -> 0 us
  local copies, waits for them, and re-layouts: 8.67 us -> 11.2 us
    pallas_call x0 -> x1, Pallas kernels: none -> 34.2 us  [local(): pl.pallas_call(functools.partial(kernel, sizes), out_shape=jax.ShapeDtype...]
    dot_general x13 -> x0, matrix products: 29.9 us -> none  [the longest x3 14 us: single_rotation(): jnp.einsum('kt,kc->tc', placing, product.reshape(-1, coeff_width), precis...]
    all_gather x3 -> x0, blocking collectives: 15.8 us -> none  [the longest x1 5.59 us: local(): nearby = lax.all_gather(with_rims, 'sub', axis=0, tiled=True)]
    ppermute x5 -> x0, starting transfers between devices: 13.4 us -> none  [the longest x3 7 us: swapped(): lax.ppermute(shard, axis, [(i, i ^ 1 << apart) for i in range(lax.axis_si...]
    unnamed x1 -> x0, blocking collectives: 11.3 us -> none
    unnamed x10 -> x27, local copies, waits for them, and re-layouts: 4.45 us -> 11.2 us
    reshape x2 -> x0, local copies, waits for them, and re-layouts: 2.39 us -> none  [the longest x1 1.57 us: single_rotation(): product.reshape(-1, coeff_width)]
    lt x3 -> x0, other arithmetic: 2.2 us -> none  [single_rotation(): is_live = (slot_numbers[None, :] < counts[:, None]).reshape(-1)]
  transfers between devices with their start and end apart: 6 -> 0, of which waited for: 0 -> 0; matrix products, arithmetic and copies ran while one was open for 44% -> 0% of each run, Pallas kernels for 0% -> 0%
where the time goes in v2:
time: 46 us; the launch traced here: 45.4 us
  Pallas kernels  34.2 us (74%)
  local copies, waits for them, and re-layouts  11.2 us (24%)
    pallas_call x1, Pallas kernels, local(): pl.pallas_call(functools.partial(kernel, sizes), out_shape=jax.ShapeDtype...  34.2 us
    unnamed x27, local copies, waits for them, and re-layouts  11.2 us

profile of v2, /device:TPU:0, one launch (start us, length us, event | category | flops | bytes accessed | tf_op | source)
XLA Modules:
  0.0 45.4 jit_solution(16669405400787450920)
XLA Ops:
  0.0 0.0 copy-start
  0.0 1.7 %copy-done = bf16[79,128,128]{2,1,0:T(8,128)(2,1)S(1)} copy-done((bf16[79,128,128]{2,1,0:T(8,128)(2,1)S(1)}, bf16[79,128,128]{2,1,0:T(8,128)(2,1)}, u32[]{:S(2)}) %copy-start) | copy-done | bytes 2588696
  1.7 0.0 copy-start.1
  1.7 0.9 %copy-done.1 = bf16[8,128,128]{2,1,0:T(8,128)(2,1)S(1)} copy-done((bf16[8,128,128]{2,1,0:T(8,128)(2,1)S(1)}, bf16[8,128,128]{2,1,0:T(8,128)(2,1)}, u32[]{:S(2)}) %copy-start.1) | copy-done | bytes 262168
  2.7 0.0 copy-start.2
  2.7 0.9 %copy-done.2 = bf16[8,128,128]{2,1,0:T(8,128)(2,1)S(1)} copy-done((bf16[8,128,128]{2,1,0:T(8,128)(2,1)S(1)}, bf16[8,128,128]{2,1,0:T(8,128)(2,1)}, u32[]{:S(2)}) %copy-start.2) | copy-done | bytes 262168
  3.6 0.0 copy-start.3
  3.6 0.8 %copy-done.3 = s32[1,79,128]{2,0,1:T(1,128)S(1)} copy-done((s32[1,79,128]{2,0,1:T(1,128)S(1)}, s32[1,79,128]{2,0,1:T(1,128)}, u32[]{:S(2)}) %copy-start.3) | copy-done | bytes 40472
  4.4 0.0 copy-start.4
  4.4 0.8 %copy-done.4 = s32[1,79,128]{2,0,1:T(1,128)S(1)} copy-done((s32[1,79,128]{2,0,1:T(1,128)S(1)}, s32[1,79,128]{2,0,1:T(1,128)}, u32[]{:S(2)}) %copy-start.4) | copy-done | bytes 40472
  5.2 0.0 copy-start.5
  5.2 0.7 %copy-done.5 = bf16[64,128]{1,0:T(8,128)(2,1)S(1)} copy-done((bf16[64,128]{1,0:T(8,128)(2,1)S(1)}, bf16[64,128]{1,0:T(8,128)(2,1)}, u32[]{:S(2)}) %copy-start.5) | copy-done | bytes 16408
  5.9 0.0 copy-start.6
  5.9 0.7 %copy-done.6 = s32[1,79,16]{1,2,0:T(8,128)S(1)} copy-done((s32[1,79,16]{1,2,0:T(8,128)S(1)}, s32[1,79,16]{1,2,0:T(8,128)}, u32[]{:S(2)}) %copy-start.6) | copy-done | bytes 5080
  6.6 0.0 copy-start.7
  6.6 0.7 %copy-done.7 = s32[1,79,16]{1,2,0:T(8,128)S(1)} copy-done((s32[1,79,16]{1,2,0:T(8,128)S(1)}, s32[1,79,16]{1,2,0:T(8,128)}, u32[]{:S(2)}) %copy-start.7) | copy-done | bytes 5080
  7.3 0.0 copy-start.8
  7.3 0.7 %copy-done.8 = s32[1,79,2]{1,2,0:T(2,128)S(1)} copy-done((s32[1,79,2]{1,2,0:T(2,128)S(1)}, s32[1,79,2]{1,2,0:T(2,128)}, u32[]{:S(2)}) %copy-start.8) | copy-done | bytes 656
  8.0 0.0 copy-start.9
  8.0 0.7 %copy-done.9 = s32[1,79,2]{1,2,0:T(2,128)S(1)} copy-done((s32[1,79,2]{1,2,0:T(2,128)S(1)}, s32[1,79,2]{1,2,0:T(2,128)}, u32[]{:S(2)}) %copy-start.9) | copy-done | bytes 656
  8.7 0.0 copy-start.10
  8.7 0.7 %copy-done.10 = s32[1,79]{1,0:T(1,128)S(1)} copy-done((s32[1,79]{1,0:T(1,128)S(1)}, s32[1,79]{1,0:T(1,128)}, u32[]{:S(2)}) %copy-start.10) | copy-done | bytes 340
  9.3 0.0 copy-start.11
  9.3 0.7 %copy-done.11 = s32[1,79]{1,0:T(1,128)S(1)} copy-done((s32[1,79]{1,0:T(1,128)S(1)}, s32[1,79]{1,0:T(1,128)}, u32[]{:S(2)}) %copy-start.11) | copy-done | bytes 340
  10.0 0.0 copy-start.12
  10.0 0.7 %copy-done.12 = s32[1,79]{1,0:T(1,128)S(1)} copy-done((s32[1,79]{1,0:T(1,128)S(1)}, s32[1,79]{1,0:T(1,128)}, u32[]{:S(2)}) %copy-start.12) | copy-done | bytes 340
  10.6 34.2 %far_field.1 = bf16[64,128]{1,0:T(8,128)(2,1)S(1)} custom-call(bf16[64,128]{1,0:T(8,128)(2,1)S(1)} %copy-done.5, bf16[79,128,128]{2,1,0:T(8,128)(2,1)S(1)} %copy-done, bf16[8,128,128]{2,1,0:T(8,128)(2,1)S(1)} %copy-done.1, bf16[8,128,128]{2,1,0:T(8,128)(2,1)S(1)} %copy-done.2, s32[79,1,128]{2,1,0:T(1,128)S(1)} %bitcast.6, s32[79,1,128]{2,1,0:T(1,128)S(1)} %bitcast.7, ...), custom_call_target="tpu_custom_call" | custom-call | tf_op jit(solution)/shard_map/far_field/pallas_call | solution.py:369
  44.8 0.6 %copy.15 = bf16[64,128]{1,0:T(8,128)(2,1)} copy(bf16[64,128]{1,0:T(8,128)(2,1)S(1)} %far_field.1) | data formatting | bytes 32768
Async XLA Ops:
  0.0 1.7 %copy-start = (bf16[79,128,128]{2,1,0:T(8,128)(2,1)S(1)}, bf16[79,128,128]{2,1,0:T(8,128)(2,1)}, u32[]{:S(2)}) copy-start(bf16[79,128,128]{2,1,0:T(8,128)(2,1)} %tr_hbm.1) | copy-start | bytes 7766020
  1.7 0.9 %copy-start.1 = (bf16[8,128,128]{2,1,0:T(8,128)(2,1)S(1)}, bf16[8,128,128]{2,1,0:T(8,128)(2,1)}, u32[]{:S(2)}) copy-start(bf16[8,128,128]{2,1,0:T(8,128)(2,1)} %up_hbm.1) | copy-start | bytes 786436
  2.7 0.9 %copy-start.2 = (bf16[8,128,128]{2,1,0:T(8,128)(2,1)S(1)}, bf16[8,128,128]{2,1,0:T(8,128)(2,1)}, u32[]{:S(2)}) copy-start(bf16[8,128,128]{2,1,0:T(8,128)(2,1)} %down_hbm.1) | copy-start | bytes 786436
  3.6 0.8 %copy-start.3 = (s32[1,79,128]{2,0,1:T(1,128)S(1)}, s32[1,79,128]{2,0,1:T(1,128)}, u32[]{:S(2)}) copy-start(s32[1,79,128]{2,0,1:T(1,128)} %param.17) | copy-start | bytes 121348
  4.4 0.8 %copy-start.4 = (s32[1,79,128]{2,0,1:T(1,128)S(1)}, s32[1,79,128]{2,0,1:T(1,128)}, u32[]{:S(2)}) copy-start(s32[1,79,128]{2,0,1:T(1,128)} %param.18) | copy-start | bytes 121348
  5.2 0.7 %copy-start.5 = (bf16[64,128]{1,0:T(8,128)(2,1)S(1)}, bf16[64,128]{1,0:T(8,128)(2,1)}, u32[]{:S(2)}) copy-start(bf16[64,128]{1,0:T(8,128)(2,1)} %mult_hbm.1) | copy-start | bytes 49156
  5.9 0.7 %copy-start.6 = (s32[1,79,16]{1,2,0:T(8,128)S(1)}, s32[1,79,16]{1,2,0:T(8,128)}, u32[]{:S(2)}) copy-start(s32[1,79,16]{1,2,0:T(8,128)} %param.20) | copy-start | bytes 15172
  6.6 0.7 %copy-start.7 = (s32[1,79,16]{1,2,0:T(8,128)S(1)}, s32[1,79,16]{1,2,0:T(8,128)}, u32[]{:S(2)}) copy-start(s32[1,79,16]{1,2,0:T(8,128)} %param.21) | copy-start | bytes 15172
  7.3 0.7 %copy-start.8 = (s32[1,79,2]{1,2,0:T(2,128)S(1)}, s32[1,79,2]{1,2,0:T(2,128)}, u32[]{:S(2)}) copy-start(s32[1,79,2]{1,2,0:T(2,128)} %param.23) | copy-start | bytes 1900
  8.0 0.7 %copy-start.9 = (s32[1,79,2]{1,2,0:T(2,128)S(1)}, s32[1,79,2]{1,2,0:T(2,128)}, u32[]{:S(2)}) copy-start(s32[1,79,2]{1,2,0:T(2,128)} %param.24) | copy-start | bytes 1900
  8.7 0.7 %copy-start.10 = (s32[1,79]{1,0:T(1,128)S(1)}, s32[1,79]{1,0:T(1,128)}, u32[]{:S(2)}) copy-start(s32[1,79]{1,0:T(1,128)} %c6_hbm.1) | copy-start | bytes 952
  9.3 0.7 %copy-start.11 = (s32[1,79]{1,0:T(1,128)S(1)}, s32[1,79]{1,0:T(1,128)}, u32[]{:S(2)}) copy-start(s32[1,79]{1,0:T(1,128)} %c5_hbm.1) | copy-start | bytes 952
  10.0 0.7 %copy-start.12 = (s32[1,79]{1,0:T(1,128)S(1)}, s32[1,79]{1,0:T(1,128)}, u32[]{:S(2)}) copy-start(s32[1,79]{1,0:T(1,128)} %c4_hbm.1) | copy-start | bytes 952

commit v3 on v2

--- a/solution.py
+++ b/solution.py
@@ -73,7 +73,7 @@
     t4_hbm, s4_hbm, c4_hbm, out_ref,
     near, coarse, mats, up, down, t6, s6, c6, t5, s5, c5, t4, s4, c4,
     wide, mt, c5t, c4t, tg6, sr6, bl6, tg5, sr5, tg4, sr4,
-    picks, places, apart, gather, parts, got,
+    picks, places, apart, gather, parts, got, choose5, choose4,
     load, near_send, near_recv, pass_send, pack_send, pack_recv, join_send, join_recv,
     part_send, part_recv,
 ):
@@ -211,9 +211,6 @@
     sr5[...] = sources(s5, 8)
     tg4[...] = keys(t4, c4, STEP, PACK)
     sr4[...] = sources(s4, STEP)
-    for o in range(n_ops, padded):
-        mats[o] = jnp.zeros(mats.shape[1:], BF16)
-    apart[...] = jnp.zeros(apart.shape, BF16)
 
     for side in range(2):
         halo_copy(side).wait_recv()
@@ -223,15 +220,36 @@
         pack_copy(k, True).wait_recv()
     for k in range(1, GROUP):
         join_copy(k, False).start()
+    slots = GROUP * n_s
+    q = lax.broadcasted_iota(jnp.int32, (slots * PACK, slots * 8), 0)
+    p = lax.broadcasted_iota(jnp.int32, (slots * PACK, slots * 8), 1)
+    choose5[...] = jnp.where(q == p // 8 * PACK + p % 8, 1.0, 0.0).astype(BF16)
+    q = lax.broadcasted_iota(jnp.int32, (slots * PACK, slots), 0)
+    p = lax.broadcasted_iota(jnp.int32, (slots * PACK, slots), 1)
+    choose4[...] = jnp.where(q == p * PACK + 8, 1.0, 0.0).astype(BF16)
+
+    apart[...] = jnp.zeros(apart.shape, BF16)
+    for o in range(n_ops, padded):
+        mats[o] = jnp.zeros(mats.shape[1:], BF16)
+    ids = lax.broadcasted_iota(jnp.int32, (boxes, cap6), 0).astype(F32).astype(BF16)
+
+    @pl.loop(0, padded // STEP)
+    def _(step):
+        for j in range(STEP):
+            lanes = pl.ds(pl.multiple_of(step * STEP * cap6 + j * cap6, cap6), cap6)
+            picks[:, lanes] = one_hot(ids, sr6[pl.ds(step * STEP + j, 1), :])
+            places[:, lanes] = one_hot(ids, tg6[pl.ds(step * STEP + j, 1), :])
+
+    r = lax.broadcasted_iota(jnp.int32, (width, width), 0)
+    c = lax.broadcasted_iota(jnp.int32, (width, width), 1)
+    eye = jnp.where(r == c, 1.0, 0.0).astype(BF16)
+
     for k in range(1, n_s):
         sub_copy(k, True).wait_recv()
     for side in range(2):
         for k in range(1, n_s):
             pass_copy(side, k, True).wait_recv()
 
-    r = lax.broadcasted_iota(jnp.int32, (width, width), 0)
-    c = lax.broadcasted_iota(jnp.int32, (width, width), 1)
-    eye = jnp.where(r == c, 1.0, 0.0).astype(BF16)
     nearby = near[...].reshape(3, boxes, width)
     for block in range(3):
         rows = dot_nt(eye, nearby[block])
@@ -241,53 +259,41 @@
             rows = jnp.where(m == n_m - 1, 0.0, rows)
         mt[pl.ds(block * width, width), :] = rows.astype(BF16)
 
-    ids = lax.broadcasted_iota(jnp.int32, (boxes, cap6), 0).astype(F32).astype(BF16)
-
     @pl.loop(0, padded // STEP)
     def _(step):
-        def mark(pair):
-            for half in range(2):
-                o = step * STEP + 2 * pair + half
-                lanes = pl.ds((2 * pair + half) * cap6, cap6)
-                picks[:, lanes] = one_hot(ids, sr6[pl.ds(o, 1), :])
-                places[:, lanes] = one_hot(ids, tg6[pl.ds(o, 1), :])
+        def both(pair):
+            start = step * STEP * cap6 + 2 * pair * cap6
+            return pl.ds(pl.multiple_of(start, 2 * cap6), 2 * cap6)
 
         def pick(pair):
-            found = dot(mt[...], picks[:, pl.ds(2 * pair * cap6, 2 * cap6)])
+            found = dot(mt[...], picks[:, both(pair)]).astype(BF16)
             for half in range(2):
                 head = bl6[pl.ds(step * STEP + 2 * pair + half, 1), :]
-                piece = found[:, half * cap6 : (half + 1) * cap6]
-                apart[pair, pl.ds(half * width, width), pl.ds(half * cap6, cap6)] = jnp.where(
-                    head == 0.0,
-                    piece[:width],
-                    jnp.where(head == 1.0, piece[width : 2 * width], piece[2 * width :]),
-                ).astype(BF16)
+                head = jnp.broadcast_to(head, (16, cap6)).astype(BF16)[None]
+                piece = found[:, half * cap6 : (half + 1) * cap6].reshape(3, width // 16, 16, cap6)
+                chosen = jnp.where(head == 1.0, piece[1], piece[2])
+                chosen = jnp.where(head == 0.0, piece[0], chosen)
+                apart[pair, pl.ds(half * width, width), pl.ds(half * cap6, cap6)] = (
+                    chosen.reshape(width, cap6)
+                )
 
         def place(pair):
-            placed = dot_nt(places[:, pl.ds(2 * pair * cap6, 2 * cap6)], apart[pair])
-            lanes = pl.ds(
-                pl.multiple_of(step * STEP * width + 2 * pair * width, 2 * width), 2 * width
-            )
+            placed = dot_nt(places[:, both(pair)], apart[pair])
+            start = step * STEP * width + 2 * pair * width
+            lanes = pl.ds(pl.multiple_of(start, 2 * width), 2 * width)
             gather[pl.ds(0, boxes), lanes] = placed.astype(BF16)
 
-        for turn in range(STEP // 2 + 2):
-            if turn >= 2:
-                place(turn - 2)
-            if 1 <= turn <= STEP // 2:
-                pick(turn - 1)
+        for turn in range(STEP // 2 + 1):
+            if turn >= 1:
+                place(turn - 1)
             if turn < STEP // 2:
-                mark(turn)
+                pick(turn)
 
     for k in range(1, GROUP):
         join_copy(k, True).wait_recv()
-    slots = GROUP * n_s
     packed = dot_nt(eye, coarse[...].reshape(slots * PACK, width)).astype(BF16)
-    q = lax.broadcasted_iota(jnp.int32, (slots * PACK, slots * 8), 0)
-    p = lax.broadcasted_iota(jnp.int32, (slots * PACK, slots * 8), 1)
-    c5t[...] = dot(packed, jnp.where(q == p // 8 * PACK + p % 8, 1.0, 0.0).astype(BF16)).astype(BF16)
-    q = lax.broadcasted_iota(jnp.int32, (slots * PACK, slots), 0)
-    p = lax.broadcasted_iota(jnp.int32, (slots * PACK, slots), 1)
-    c4t[...] = dot(packed, jnp.where(q == p * PACK + 8, 1.0, 0.0).astype(BF16)).astype(BF16)
+    c5t[...] = dot(packed, choose5[...]).astype(BF16)
+    c4t[...] = dot(packed, choose4[...]).astype(BF16)
 
     def numbers(height, lanes):
         return lax.broadcasted_iota(jnp.int32, (height, lanes), 0).astype(F32).astype(BF16)
@@ -369,7 +375,7 @@
     return pl.pallas_call(
         functools.partial(kernel, sizes),
         out_shape=jax.ShapeDtypeStruct((quarter, width), BF16),
-        in_specs=[pl.BlockSpec(memory_space=pl.ANY)] * 13,
+        in_specs=[pl.BlockSpec(memory_space=pltpu.HBM)] * 13,
         out_specs=pl.BlockSpec(memory_space=pltpu.VMEM),
         scratch_shapes=[
             pltpu.VMEM((3 * n_s, quarter, width), BF16),
@@ -389,12 +395,14 @@
             pltpu.VMEM((padded // 8, 8 * cap5), F32),
             pltpu.VMEM((padded // STEP, STEP * cap4), F32),
             pltpu.VMEM((padded // STEP, STEP * cap4), F32),
-            pltpu.VMEM((boxes, STEP * cap6), BF16),
-            pltpu.VMEM((boxes, STEP * cap6), BF16),
+            pltpu.VMEM((boxes, padded * cap6), BF16),
+            pltpu.VMEM((boxes, padded * cap6), BF16),
             pltpu.VMEM((STEP // 2, 2 * width, 2 * cap6), BF16),
             pltpu.VMEM((rows, padded * width), BF16),
             pltpu.VMEM((n_s, quarter + PACK, width), BF16),
             pltpu.VMEM((n_s, quarter + PACK, width), BF16),
+            pltpu.VMEM((slots * PACK, slots * 8), BF16),
+            pltpu.VMEM((slots * PACK, slots), BF16),
             sems((13,)),
             sems((2 + n_s,)),
             sems((3 * n_s,)),
@@ -407,7 +415,7 @@
             sems((n_s,)),
         ],
         compiler_params=pltpu.CompilerParams(
-            collective_id=0, has_side_effects=True, vmem_limit_bytes=48 * 1024 * 1024
+            collective_id=0, has_side_effects=True, vmem_limit_bytes=63 * 1024 * 1024
         ),
         name="far_field",
     )(mult, trans, up, down, t6, s6, c6, t5, s5, c5, t4, s4, c4)

time: 46 us -> 36.2 us (0.79)
  local copies, waits for them, and re-layouts: 11.2 us -> 1.32 us
    unnamed x27 -> x1, local copies, waits for them, and re-layouts: 11.2 us -> 1.32 us
where the time goes in v3:
time: 36.2 us; the launch traced here: 35.9 us
  Pallas kernels  34.6 us (96%)
  local copies, waits for them, and re-layouts  1.32 us (4%)
    pallas_call x1, Pallas kernels, local(): pl.pallas_call(functools.partial(kernel, sizes), out_shape=jax.ShapeDtype...  34.6 us
    unnamed x1, local copies, waits for them, and re-layouts  1.32 us

profile of v3, /device:TPU:0, one launch (start us, length us, event | category | flops | bytes accessed | tf_op | source)
XLA Modules:
  0.0 35.9 jit_solution(9300964507824320536)
XLA Ops:
  0.0 34.6 %far_field.1 = bf16[64,128]{1,0:T(8,128)(2,1)} custom-call(bf16[64,128]{1,0:T(8,128)(2,1)} %mult_hbm.1, bf16[79,128,128]{2,1,0:T(8,128)(2,1)} %tr_hbm.1, bf16[8,128,128]{2,1,0:T(8,128)(2,1)} %up_hbm.1, bf16[8,128,128]{2,1,0:T(8,128)(2,1)} %down_hbm.1, s32[79,1,128]{2,1,0:T(1,128)} %bitcast.6, s32[79,1,128]{2,1,0:T(1,128)} %bitcast.7, s32[1,79]{1,0:T(1,128)} %c6_hbm.1, ...), custom_call_target="tpu_custom_call" | custom-call | tf_op jit(solution)/shard_map/far_field/pallas_call | solution.py:375
  34.6 1.3 %copy.15 = bf16[64,128]{1,0:T(8,128)(2,1)} copy(bf16[64,128]{1,0:T(8,128)(2,1)} %far_field.1) | data formatting | bytes 32768

commit v4 on v3

--- a/solution.py
+++ b/solution.py
@@ -73,7 +73,8 @@
     t4_hbm, s4_hbm, c4_hbm, out_ref,
     near, coarse, mats, up, down, t6, s6, c6, t5, s5, c5, t4, s4, c4,
     wide, mt, c5t, c4t, tg6, sr6, bl6, tg5, sr5, tg4, sr4,
-    picks, places, apart, gather, parts, got, choose5, choose4,
+    picks, places, apart, gather, turned, products, parts, got, choose5,
+    choose4,
     load, near_send, near_recv, pass_send, pack_send, pack_recv, join_send, join_recv,
     part_send, part_recv,
 ):
@@ -244,6 +245,16 @@
     c = lax.broadcasted_iota(jnp.int32, (width, width), 1)
     eye = jnp.where(r == c, 1.0, 0.0).astype(BF16)
 
+    loads[11].wait()
+
+    @pl.loop(0, padded // STEP)
+    def _(step):
+        for pair in range(STEP // 2):
+            both = mats[pl.ds(step * STEP + 2 * pair, 2)].reshape(2 * width, width)
+            start = step * STEP * width + 2 * pair * width
+            lanes = pl.ds(pl.multiple_of(start, 2 * width), 2 * width)
+            turned[:, lanes] = dot_nt(eye, both).astype(BF16)
+
     for k in range(1, n_s):
         sub_copy(k, True).wait_recv()
     for side in range(2):
@@ -259,34 +270,38 @@
             rows = jnp.where(m == n_m - 1, 0.0, rows)
         mt[pl.ds(block * width, width), :] = rows.astype(BF16)
 
+    quads = STEP // 4
+
     @pl.loop(0, padded // STEP)
     def _(step):
-        def both(pair):
-            start = step * STEP * cap6 + 2 * pair * cap6
-            return pl.ds(pl.multiple_of(start, 2 * cap6), 2 * cap6)
-
-        def pick(pair):
-            found = dot(mt[...], picks[:, both(pair)]).astype(BF16)
-            for half in range(2):
-                head = bl6[pl.ds(step * STEP + 2 * pair + half, 1), :]
+        def pick(quad):
+            start = step * STEP * cap6 + 4 * quad * cap6
+            lanes = pl.ds(pl.multiple_of(start, 4 * cap6), 4 * cap6)
+            found = dot(mt[...], picks[:, lanes]).astype(BF16)
+            for k in range(4):
+                o = 4 * quad + k
+                head = bl6[pl.ds(step * STEP + o, 1), :]
                 head = jnp.broadcast_to(head, (16, cap6)).astype(BF16)[None]
-                piece = found[:, half * cap6 : (half + 1) * cap6].reshape(3, width // 16, 16, cap6)
+                piece = found[:, k * cap6 : (k + 1) * cap6].reshape(3, width // 16, 16, cap6)
                 chosen = jnp.where(head == 1.0, piece[1], piece[2])
                 chosen = jnp.where(head == 0.0, piece[0], chosen)
-                apart[pair, pl.ds(half * width, width), pl.ds(half * cap6, cap6)] = (
+                half = o % 2
+                apart[o // 2, pl.ds(half * width, width), pl.ds(half * cap6, cap6)] = (
                     chosen.reshape(width, cap6)
                 )
 
-        def place(pair):
-            placed = dot_nt(places[:, both(pair)], apart[pair])
+        def translate(pair):
             start = step * STEP * width + 2 * pair * width
             lanes = pl.ds(pl.multiple_of(start, 2 * width), 2 * width)
-            gather[pl.ds(0, boxes), lanes] = placed.astype(BF16)
-
-        for turn in range(STEP // 2 + 1):
+            start = step * STEP * cap6 + 2 * pair * cap6
+            slots = pl.ds(pl.multiple_of(start, 2 * cap6), 2 * cap6)
+            products[:, slots] = dot(turned[:, lanes], apart[pair]).astype(BF16)
+
+        for turn in range(quads + 1):
             if turn >= 1:
-                place(turn - 1)
-            if turn < STEP // 2:
+                translate(2 * turn - 2)
+                translate(2 * turn - 1)
+            if turn < quads:
                 pick(turn)
 
     for k in range(1, GROUP):
@@ -301,33 +316,33 @@
     source5, target5 = numbers(slots * 8, 8 * cap5), numbers(8 * fives, 8 * cap5)
     source4, target4 = numbers(slots, STEP * cap4), numbers(STEP * PACK, STEP * cap4)
 
-    @pl.loop(0, padded // STEP)
-    def _(step):
-        def at(o):
-            return pl.ds(pl.multiple_of(step * STEP * width + o * width, width), width)
+    for step in range(padded // STEP):
+
+        def at(o, step=step):
+            return pl.ds((step * STEP + o) * width, width)
 
         for half in range(STEP // 8):
             row = step * (STEP // 8) + half
             found = dot(c5t[...], one_hot(source5, sr5[pl.ds(row, 1), :])).astype(BF16)
             placed = dot_nt(one_hot(target5, tg5[pl.ds(row, 1), :]), found).astype(BF16)
             for o in range(8):
-                gather[pl.ds(boxes, fives), at(half * 8 + o)] = placed[o * fives : (o + 1) * fives]
+                gather[pl.ds(0, fives), at(half * 8 + o)] = placed[o * fives : (o + 1) * fives]
         found = dot(c4t[...], one_hot(source4, sr4[pl.ds(step, 1), :])).astype(BF16)
         placed = dot_nt(one_hot(target4, tg4[pl.ds(step, 1), :]), found).astype(BF16)
         for o in range(STEP):
-            gather[pl.ds(boxes + fives, PACK), at(o)] = placed[o * PACK : (o + 1) * PACK]
-
-    loads[11].wait()
-    total = dot(gather[...], mats[...].reshape(padded * width, width))
+            gather[pl.ds(fives, PACK), at(o)] = placed[o * PACK : (o + 1) * PACK]
+
+    total = dot_nt(products[...], places[...]).T
+    low = dot(gather[...], mats[...].reshape(padded * width, width))
 
     six, five, four = boxes // n_s, fives // n_s, fours // n_s
     for part in range(n_s):
         parts[part, pl.ds(0, six), :] = total[part * six : (part + 1) * six].astype(BF16)
-        low = boxes + fives + part * four
+        last = fives + part * four
         tail = jnp.concatenate(
             [
-                total[boxes + part * five : boxes + (part + 1) * five] * 0.5,
-                total[low : low + four] * 0.25,
+                low[part * five : (part + 1) * five] * 0.5,
+                low[last : last + four] * 0.25,
                 jnp.zeros((PACK - five - four, width), F32),
             ],
             axis=0,
@@ -366,7 +381,7 @@
     slots = GROUP * n_s
     n_ops = trans.shape[0]
     padded = -(-n_ops // STEP) * STEP
-    rows = boxes + boxes // 8 + PACK
+    rows = boxes // 8 + PACK
     cap6, cap5, cap4 = t6.shape[2], t5.shape[2], t4.shape[2]
     t6, s6 = jnp.swapaxes(t6, 0, 1), jnp.swapaxes(s6, 0, 1)
     t5, s5, t4, s4 = (jnp.swapaxes(x, 1, 2) for x in (t5, s5, t4, s4))
@@ -399,6 +414,8 @@
             pltpu.VMEM((boxes, padded * cap6), BF16),
             pltpu.VMEM((STEP // 2, 2 * width, 2 * cap6), BF16),
             pltpu.VMEM((rows, padded * width), BF16),
+            pltpu.VMEM((width, padded * width), BF16),
+            pltpu.VMEM((width, padded * cap6), BF16),
             pltpu.VMEM((n_s, quarter + PACK, width), BF16),
             pltpu.VMEM((n_s, quarter + PACK, width), BF16),
             pltpu.VMEM((slots * PACK, slots * 8), BF16),

time: 36.2 us -> 30.5 us (0.84)
  Pallas kernels: 34.6 us -> 28.9 us
    pallas_call x1, Pallas kernels: 34.6 us -> 28.9 us  [local(): pl.pallas_call(functools.partial(kernel, sizes), out_shape=jax.ShapeDtype...]
where the time goes in v4:
time: 30.5 us; the launch traced here: 30.2 us
  Pallas kernels  28.9 us (95%)
  local copies, waits for them, and re-layouts  1.32 us (4%)
    pallas_call x1, Pallas kernels, local(): pl.pallas_call(functools.partial(kernel, sizes), out_shape=jax.ShapeDtype...  28.9 us
    unnamed x1, local copies, waits for them, and re-layouts  1.32 us

profile of v4, /device:TPU:0, one launch (start us, length us, event | category | flops | bytes accessed | tf_op | source)
XLA Modules:
  0.0 30.2 jit_solution(1835921281909455579)
XLA Ops:
  0.0 28.9 %far_field.1 = bf16[64,128]{1,0:T(8,128)(2,1)} custom-call(bf16[64,128]{1,0:T(8,128)(2,1)} %mult_hbm.1, bf16[79,128,128]{2,1,0:T(8,128)(2,1)} %tr_hbm.1, bf16[8,128,128]{2,1,0:T(8,128)(2,1)} %up_hbm.1, bf16[8,128,128]{2,1,0:T(8,128)(2,1)} %down_hbm.1, s32[79,1,128]{2,1,0:T(1,128)} %bitcast.6, s32[79,1,128]{2,1,0:T(1,128)} %bitcast.7, s32[1,79]{1,0:T(1,128)} %c6_hbm.1, ...), custom_call_target="tpu_custom_call" | custom-call | tf_op jit(solution)/shard_map/far_field/pallas_call | solution.py:390
  28.9 1.3 %copy.15 = bf16[64,128]{1,0:T(8,128)(2,1)} copy(bf16[64,128]{1,0:T(8,128)(2,1)} %far_field.1) | data formatting | bytes 32768

commit v5 on v4

--- a/solution.py
+++ b/solution.py
@@ -239,7 +239,6 @@
         for j in range(STEP):
             lanes = pl.ds(pl.multiple_of(step * STEP * cap6 + j * cap6, cap6), cap6)
             picks[:, lanes] = one_hot(ids, sr6[pl.ds(step * STEP + j, 1), :])
-            places[:, lanes] = one_hot(ids, tg6[pl.ds(step * STEP + j, 1), :])
 
     r = lax.broadcasted_iota(jnp.int32, (width, width), 0)
     c = lax.broadcasted_iota(jnp.int32, (width, width), 1)
@@ -289,6 +288,8 @@
                 apart[o // 2, pl.ds(half * width, width), pl.ds(half * cap6, cap6)] = (
                     chosen.reshape(width, cap6)
                 )
+                lanes = pl.ds(pl.multiple_of((step * STEP + o) * cap6, cap6), cap6)
+                places[:, lanes] = one_hot(ids, tg6[pl.ds(step * STEP + o, 1), :])
 
         def translate(pair):
             start = step * STEP * width + 2 * pair * width
@@ -332,8 +333,13 @@
         for o in range(STEP):
             gather[pl.ds(fives, PACK), at(o)] = placed[o * PACK : (o + 1) * PACK]
 
-    total = dot_nt(products[...], places[...]).T
-    low = dot(gather[...], mats[...].reshape(padded * width, width))
+    total, low = 0.0, 0.0
+    for step in range(padded // STEP):
+        lanes = pl.ds(step * STEP * cap6, STEP * cap6)
+        total = total + dot_nt(products[:, lanes], places[:, lanes])
+        ops = mats[pl.ds(step * STEP, STEP)].reshape(STEP * width, width)
+        low = low + dot(gather[:, pl.ds(step * STEP * width, STEP * width)], ops)
+    total = total.T
 
     six, five, four = boxes // n_s, fives // n_s, fours // n_s
     for part in range(n_s):

time: 30.5 us -> 30.3 us (level)
  no operation moved by 1% of the time
where the time goes in v5:
time: 30.3 us; the launch traced here: 30 us
  Pallas kernels  28.6 us (94%)
  local copies, waits for them, and re-layouts  1.32 us (4%)
    pallas_call x1, Pallas kernels, local(): pl.pallas_call(functools.partial(kernel, sizes), out_shape=jax.ShapeDtype...  28.6 us
    unnamed x1, local copies, waits for them, and re-layouts  1.32 us

profile of v5, /device:TPU:0, one launch (start us, length us, event | category | flops | bytes accessed | tf_op | source)
XLA Modules:
  0.0 30.0 jit_solution(2722112420896790547)
XLA Ops:
  0.0 28.6 %far_field.1 = bf16[64,128]{1,0:T(8,128)(2,1)} custom-call(bf16[64,128]{1,0:T(8,128)(2,1)} %mult_hbm.1, bf16[79,128,128]{2,1,0:T(8,128)(2,1)} %tr_hbm.1, bf16[8,128,128]{2,1,0:T(8,128)(2,1)} %up_hbm.1, bf16[8,128,128]{2,1,0:T(8,128)(2,1)} %down_hbm.1, s32[79,1,128]{2,1,0:T(1,128)} %bitcast.6, s32[79,1,128]{2,1,0:T(1,128)} %bitcast.7, s32[1,79]{1,0:T(1,128)} %c6_hbm.1, ...), custom_call_target="tpu_custom_call" | custom-call | tf_op jit(solution)/shard_map/far_field/pallas_call | solution.py:396
  28.6 1.3 %copy.15 = bf16[64,128]{1,0:T(8,128)(2,1)} copy(bf16[64,128]{1,0:T(8,128)(2,1)} %far_field.1) | data formatting | bytes 32768

commit v6 on v5

--- a/solution.py
+++ b/solution.py
@@ -73,10 +73,10 @@
     t4_hbm, s4_hbm, c4_hbm, out_ref,
     near, coarse, mats, up, down, t6, s6, c6, t5, s5, c5, t4, s4, c4,
     wide, mt, c5t, c4t, tg6, sr6, bl6, tg5, sr5, tg4, sr4,
-    picks, places, apart, gather, turned, products, parts, got, choose5,
-    choose4,
+    picks, places, apart, gather, turned, products, parts, got, tails,
+    got_tails, choose4,
     load, near_send, near_recv, pass_send, pack_send, pack_recv, join_send, join_recv,
-    part_send, part_recv,
+    part_send, part_recv, tail_send, tail_recv,
 ):
     n_m, n_s = sizes
     n_ops, width = tr_hbm.shape[0], tr_hbm.shape[2]
@@ -165,6 +165,12 @@
             parts.at[other], got.at[k], part_send.at[k], part_recv.at[k], (m, other)
         )
 
+    def tail_copy(k):
+        other = wrapped(s + k, n_s)
+        return remote(
+            tails.at[other], got_tails.at[k], tail_send.at[k], tail_recv.at[k], (m, other)
+        )
+
     loads[0].wait()
     pl.semaphore_wait(barrier, expected)
     for side in range(2):
@@ -222,11 +228,8 @@
     for k in range(1, GROUP):
         join_copy(k, False).start()
     slots = GROUP * n_s
-    q = lax.broadcasted_iota(jnp.int32, (slots * PACK, slots * 8), 0)
-    p = lax.broadcasted_iota(jnp.int32, (slots * PACK, slots * 8), 1)
-    choose5[...] = jnp.where(q == p // 8 * PACK + p % 8, 1.0, 0.0).astype(BF16)
-    q = lax.broadcasted_iota(jnp.int32, (slots * PACK, slots), 0)
-    p = lax.broadcasted_iota(jnp.int32, (slots * PACK, slots), 1)
+    p = lax.broadcasted_iota(jnp.int32, (slots, slots * PACK), 0)
+    q = lax.broadcasted_iota(jnp.int32, (slots, slots * PACK), 1)
     choose4[...] = jnp.where(q == p * PACK + 8, 1.0, 0.0).astype(BF16)
 
     apart[...] = jnp.zeros(apart.shape, BF16)
@@ -268,6 +271,56 @@
         if block == 2:
             rows = jnp.where(m == n_m - 1, 0.0, rows)
         mt[pl.ds(block * width, width), :] = rows.astype(BF16)
+
+    for k in range(1, GROUP):
+        join_copy(k, True).wait_recv()
+    message = coarse[...].reshape(slots, PACK, width)
+    rows5 = message.astype(F32)[:, :8, :].reshape(slots * 8, width).astype(BF16)
+    c5t[...] = dot_nt(eye, rows5).astype(BF16)
+    rows4 = dot(choose4[...], message.reshape(slots * PACK, width)).astype(BF16)
+    c4t[...] = dot_nt(eye, rows4).astype(BF16)
+
+    def numbers(height, lanes):
+        return lax.broadcasted_iota(jnp.int32, (height, lanes), 0).astype(F32).astype(BF16)
+
+    source5, target5 = numbers(slots * 8, 8 * cap5), numbers(8 * fives, 8 * cap5)
+    source4, target4 = numbers(slots, STEP * cap4), numbers(STEP * PACK, STEP * cap4)
+
+    for step in range(padded // STEP):
+
+        def at(o, step=step):
+            return pl.ds((step * STEP + o) * width, width)
+
+        for half in range(STEP // 8):
+            row = step * (STEP // 8) + half
+            found = dot(c5t[...], one_hot(source5, sr5[pl.ds(row, 1), :])).astype(BF16)
+            placed = dot_nt(one_hot(target5, tg5[pl.ds(row, 1), :]), found).astype(BF16)
+            for o in range(8):
+                gather[pl.ds(0, fives), at(half * 8 + o)] = placed[o * fives : (o + 1) * fives]
+        found = dot(c4t[...], one_hot(source4, sr4[pl.ds(step, 1), :])).astype(BF16)
+        placed = dot_nt(one_hot(target4, tg4[pl.ds(step, 1), :]), found).astype(BF16)
+        for o in range(STEP):
+            gather[pl.ds(fives, PACK), at(o)] = placed[o * PACK : (o + 1) * PACK]
+
+    low = 0.0
+    for step in range(padded // STEP):
+        ops = mats[pl.ds(step * STEP, STEP)].reshape(STEP * width, width)
+        low = low + dot(gather[:, pl.ds(step * STEP * width, STEP * width)], ops)
+
+    six, five, four = boxes // n_s, fives // n_s, fours // n_s
+    for part in range(n_s):
+        last = fives + part * four
+        tail = jnp.concatenate(
+            [
+                low[part * five : (part + 1) * five] * 0.5,
+                low[last : last + four] * 0.25,
+                jnp.zeros((PACK - five - four, width), F32),
+            ],
+            axis=0,
+        )
+        tails[part] = tail.astype(BF16)
+    for k in range(1, n_s):
+        tail_copy(k).start()
 
     quads = STEP // 4
 
@@ -305,68 +358,30 @@
             if turn < quads:
                 pick(turn)
 
-    for k in range(1, GROUP):
-        join_copy(k, True).wait_recv()
-    packed = dot_nt(eye, coarse[...].reshape(slots * PACK, width)).astype(BF16)
-    c5t[...] = dot(packed, choose5[...]).astype(BF16)
-    c4t[...] = dot(packed, choose4[...]).astype(BF16)
-
-    def numbers(height, lanes):
-        return lax.broadcasted_iota(jnp.int32, (height, lanes), 0).astype(F32).astype(BF16)
-
-    source5, target5 = numbers(slots * 8, 8 * cap5), numbers(8 * fives, 8 * cap5)
-    source4, target4 = numbers(slots, STEP * cap4), numbers(STEP * PACK, STEP * cap4)
-
-    for step in range(padded // STEP):
-
-        def at(o, step=step):
-            return pl.ds((step * STEP + o) * width, width)
-
-        for half in range(STEP // 8):
-            row = step * (STEP // 8) + half
-            found = dot(c5t[...], one_hot(source5, sr5[pl.ds(row, 1), :])).astype(BF16)
-            placed = dot_nt(one_hot(target5, tg5[pl.ds(row, 1), :]), found).astype(BF16)
-            for o in range(8):
-                gather[pl.ds(0, fives), at(half * 8 + o)] = placed[o * fives : (o + 1) * fives]
-        found = dot(c4t[...], one_hot(source4, sr4[pl.ds(step, 1), :])).astype(BF16)
-        placed = dot_nt(one_hot(target4, tg4[pl.ds(step, 1), :]), found).astype(BF16)
-        for o in range(STEP):
-            gather[pl.ds(fives, PACK), at(o)] = placed[o * PACK : (o + 1) * PACK]
-
-    total, low = 0.0, 0.0
+    total = 0.0
     for step in range(padded // STEP):
         lanes = pl.ds(step * STEP * cap6, STEP * cap6)
         total = total + dot_nt(products[:, lanes], places[:, lanes])
-        ops = mats[pl.ds(step * STEP, STEP)].reshape(STEP * width, width)
-        low = low + dot(gather[:, pl.ds(step * STEP * width, STEP * width)], ops)
     total = total.T
-
-    six, five, four = boxes // n_s, fives // n_s, fours // n_s
     for part in range(n_s):
-        parts[part, pl.ds(0, six), :] = total[part * six : (part + 1) * six].astype(BF16)
-        last = fives + part * four
-        tail = jnp.concatenate(
-            [
-                low[part * five : (part + 1) * five] * 0.5,
-                low[last : last + four] * 0.25,
-                jnp.zeros((PACK - five - four, width), F32),
-            ],
-            axis=0,
-        )
-        parts[part, pl.ds(six, PACK), :] = tail.astype(BF16)
+        parts[part] = total[part * six : (part + 1) * six].astype(BF16)
     for k in range(1, n_s):
         part_copy(k).start()
     loads[12].wait()
+    below = tails[s].astype(F32)
+    for k in range(1, n_s):
+        tail_copy(k).wait_recv()
+        below = below + got_tails[k].astype(F32)
+    row = below[five : five + 1, :].astype(BF16)
+    spread = [dot(row, down[c]) for c in range(8)]
+    mid = (below[:five, :] + jnp.concatenate(spread, axis=0)).astype(BF16)
+    for c in range(8):
+        wide[pl.ds(c, six // 8, stride=8), :] = dot(mid, down[c])
     whole = parts[s].astype(F32)
     for k in range(1, n_s):
         part_copy(k).wait_recv()
         whole = whole + got[k].astype(F32)
-    row = whole[six + five : six + five + 1, :].astype(BF16)
-    spread = [dot(row, down[c]) for c in range(8)]
-    mid = (whole[six : six + five, :] + jnp.concatenate(spread, axis=0)).astype(BF16)
-    for c in range(8):
-        wide[pl.ds(c, six // 8, stride=8), :] = dot(mid, down[c])
-    out_ref[...] = (wide[...] + whole[:six, :]).astype(BF16)
+    out_ref[...] = (wide[...] + whole).astype(BF16)
 
     for side in range(2):
         halo_copy(side).wait_send()
@@ -376,6 +391,7 @@
         sub_copy(k, False).wait_send()
         pack_copy(k, False).wait_send()
         part_copy(k).wait_send()
+        tail_copy(k).wait_send()
     for k in range(1, GROUP):
         join_copy(k, False).wait_send()
 
@@ -422,10 +438,11 @@
             pltpu.VMEM((rows, padded * width), BF16),
             pltpu.VMEM((width, padded * width), BF16),
             pltpu.VMEM((width, padded * cap6), BF16),
-            pltpu.VMEM((n_s, quarter + PACK, width), BF16),
-            pltpu.VMEM((n_s, quarter + PACK, width), BF16),
-            pltpu.VMEM((slots * PACK, slots * 8), BF16),
-            pltpu.VMEM((slots * PACK, slots), BF16),
+            pltpu.VMEM((n_s, quarter, width), BF16),
+            pltpu.VMEM((n_s, quarter, width), BF16),
+            pltpu.VMEM((n_s, PACK, width), BF16),
+            pltpu.VMEM((n_s, PACK, width), BF16),
+            pltpu.VMEM((slots, slots * PACK), BF16),
             sems((13,)),
             sems((2 + n_s,)),
             sems((3 * n_s,)),
@@ -434,6 +451,8 @@
             sems((n_s,)),
             sems((GROUP,)),
             sems((GROUP,)),
+            sems((n_s,)),
+            sems((n_s,)),
             sems((n_s,)),
             sems((n_s,)),
         ],

time: 30.3 us -> 32.3 us (1.066)
  Pallas kernels: 28.6 us -> 30.7 us
    pallas_call x1, Pallas kernels: 28.6 us -> 30.7 us  [local(): pl.pallas_call(functools.partial(kernel, sizes), out_shape=jax.ShapeDtype...]
where the time goes in v6:
time: 32.3 us; the launch traced here: 32 us
  Pallas kernels  30.7 us (95%)
  local copies, waits for them, and re-layouts  1.32 us (4%)
    pallas_call x1, Pallas kernels, local(): pl.pallas_call(functools.partial(kernel, sizes), out_shape=jax.ShapeDtype...  30.7 us
    unnamed x1, local copies, waits for them, and re-layouts  1.32 us

profile of v6, /device:TPU:0, one launch (start us, length us, event | category | flops | bytes accessed | tf_op | source)
XLA Modules:
  0.0 32.0 jit_solution(5190246621088525640)
XLA Ops:
  0.0 30.7 %far_field.1 = bf16[64,128]{1,0:T(8,128)(2,1)} custom-call(bf16[64,128]{1,0:T(8,128)(2,1)} %mult_hbm.1, bf16[79,128,128]{2,1,0:T(8,128)(2,1)} %tr_hbm.1, bf16[8,128,128]{2,1,0:T(8,128)(2,1)} %up_hbm.1, bf16[8,128,128]{2,1,0:T(8,128)(2,1)} %down_hbm.1, s32[79,1,128]{2,1,0:T(1,128)} %bitcast.6, s32[79,1,128]{2,1,0:T(1,128)} %bitcast.7, s32[1,79]{1,0:T(1,128)} %c6_hbm.1, ...), custom_call_target="tpu_custom_call" | custom-call | tf_op jit(solution)/shard_map/far_field/pallas_call | solution.py:412
  30.7 1.3 %copy.15 = bf16[64,128]{1,0:T(8,128)(2,1)} copy(bf16[64,128]{1,0:T(8,128)(2,1)} %far_field.1) | data formatting | bytes 32768

commit v7 on v5

--- a/solution.py
+++ b/solution.py
@@ -165,17 +165,6 @@
             parts.at[other], got.at[k], part_send.at[k], part_recv.at[k], (m, other)
         )
 
-    loads[0].wait()
-    pl.semaphore_wait(barrier, expected)
-    for side in range(2):
-        halo_copy(side).start()
-    for k in range(1, n_s):
-        sub_copy(k, False).start()
-    loads[1].wait()
-    coarse[here, s] = upward_rows(near[n_s + s], up[...], wide)
-    for k in range(1, n_s):
-        pack_copy(k, False).start()
-
     for copy in loads[2:11]:
         copy.wait()
 
@@ -212,6 +201,28 @@
     sr5[...] = sources(s5, 8)
     tg4[...] = keys(t4, c4, STEP, PACK)
     sr4[...] = sources(s4, STEP)
+
+    loads[0].wait()
+    pl.semaphore_wait(barrier, expected)
+    for side in range(2):
+        halo_copy(side).start()
+    for k in range(1, n_s):
+        sub_copy(k, False).start()
+    loads[1].wait()
+    coarse[here, s] = upward_rows(near[n_s + s], up[...], wide)
+    for k in range(1, n_s):
+        pack_copy(k, False).start()
+
+    apart[...] = jnp.zeros(apart.shape, BF16)
+    for o in range(n_ops, padded):
+        mats[o] = jnp.zeros(mats.shape[1:], BF16)
+    ids = lax.broadcasted_iota(jnp.int32, (boxes, cap6), 0).astype(F32).astype(BF16)
+
+    @pl.loop(0, padded // STEP)
+    def _(step):
+        for j in range(STEP):
+            lanes = pl.ds(pl.multiple_of(step * STEP * cap6 + j * cap6, cap6), cap6)
+            picks[:, lanes] = one_hot(ids, sr6[pl.ds(step * STEP + j, 1), :])
 
     for side in range(2):
         halo_copy(side).wait_recv()
@@ -228,17 +239,6 @@
     q = lax.broadcasted_iota(jnp.int32, (slots * PACK, slots), 0)
     p = lax.broadcasted_iota(jnp.int32, (slots * PACK, slots), 1)
     choose4[...] = jnp.where(q == p * PACK + 8, 1.0, 0.0).astype(BF16)
-
-    apart[...] = jnp.zeros(apart.shape, BF16)
-    for o in range(n_ops, padded):
-        mats[o] = jnp.zeros(mats.shape[1:], BF16)
-    ids = lax.broadcasted_iota(jnp.int32, (boxes, cap6), 0).astype(F32).astype(BF16)
-
-    @pl.loop(0, padded // STEP)
-    def _(step):
-        for j in range(STEP):
-            lanes = pl.ds(pl.multiple_of(step * STEP * cap6 + j * cap6, cap6), cap6)
-            picks[:, lanes] = one_hot(ids, sr6[pl.ds(step * STEP + j, 1), :])
 
     r = lax.broadcasted_iota(jnp.int32, (width, width), 0)
     c = lax.broadcasted_iota(jnp.int32, (width, width), 1)

time: 30.3 us -> 30.5 us (level)
  Pallas kernels: 28.6 us -> 29 us
    pallas_call x1, Pallas kernels: 28.6 us -> 29 us  [local(): pl.pallas_call(functools.partial(kernel, sizes), out_shape=jax.ShapeDtype...]
where the time goes in v7:
time: 30.5 us; the launch traced here: 30.3 us
  Pallas kernels  29 us (95%)
  local copies, waits for them, and re-layouts  1.32 us (4%)
    pallas_call x1, Pallas kernels, local(): pl.pallas_call(functools.partial(kernel, sizes), out_shape=jax.ShapeDtype...  29 us
    unnamed x1, local copies, waits for them, and re-layouts  1.32 us

profile of v7, /device:TPU:0, one launch (start us, length us, event | category | flops | bytes accessed | tf_op | source)
XLA Modules:
  0.0 30.3 jit_solution(9129653069009125964)
XLA Ops:
  0.0 29.0 %far_field.1 = bf16[64,128]{1,0:T(8,128)(2,1)} custom-call(bf16[64,128]{1,0:T(8,128)(2,1)} %mult_hbm.1, bf16[79,128,128]{2,1,0:T(8,128)(2,1)} %tr_hbm.1, bf16[8,128,128]{2,1,0:T(8,128)(2,1)} %up_hbm.1, bf16[8,128,128]{2,1,0:T(8,128)(2,1)} %down_hbm.1, s32[79,1,128]{2,1,0:T(1,128)} %bitcast.6, s32[79,1,128]{2,1,0:T(1,128)} %bitcast.7, s32[1,79]{1,0:T(1,128)} %c6_hbm.1, ...), custom_call_target="tpu_custom_call" | custom-call | tf_op jit(solution)/shard_map/far_field/pallas_call | solution.py:396
  29.0 1.3 %copy.15 = bf16[64,128]{1,0:T(8,128)(2,1)} copy(bf16[64,128]{1,0:T(8,128)(2,1)} %far_field.1) | data formatting | bytes 32768
